TPU v7x, 32 devices: a whole 2x2x4 slice. The times are simulated.
32 devices in a mesh: seq: 8 (over z, y), tp: 4 (over x, core).
Axes of the slice: x: 2, y: 2, z: 4, core: 2. Of those that a mesh axis runs over, the one named last changes fastest.
Arguments:
- stream_in: bfloat16 [4, 2048, 1024], P(None, 'seq'), may hold values from -6 to 6
- norm_gain: bfloat16 [2, 1024], replicated, may hold values from 0.099609375 to 1.8984375
- in_proj: bfloat16 [2, 1024, 3, 1024], P(None, None, None, 'tp'), may hold values from -0.1875 to 0.1875
- conv_taps: bfloat16 [2, 3, 1024], P(None, None, 'tp'), may hold values from -3.5 to 3.5
- out_proj: bfloat16 [2, 1024, 1024], P(None, 'tp'), may hold values from -0.1875 to 0.1875
- ffn_gain: bfloat16 [2, 1024], replicated, may hold values from 0.099609375 to 1.8984375
- gate_proj: bfloat16 [2, 1024, 4608], P(None, None, 'tp'), may hold values from -0.1875 to 0.1875
- up_proj: bfloat16 [2, 1024, 4608], P(None, None, 'tp'), may hold values from -0.1875 to 0.1875
- down_proj: bfloat16 [2, 4608, 1024], P(None, 'tp'), may hold values from -0.09375 to 0.09375
- out_grad: bfloat16 [4, 2048, 1024], P(None, 'seq'), may hold values from -6 to 6
Outputs:
- stream_out: bfloat16 [4, 2048, 1024], P(None, 'seq')
- stream_grad: float32 [4, 2048, 1024], P(None, 'seq')
- norm_gain_grad: float32 [2, 1024], P(None, 'tp')
- in_proj_grad: float32 [2, 1024, 3, 1024], P(None, 'seq', None, 'tp')
- conv_grad: float32 [2, 3, 1024], P(None, None, 'tp')
- out_proj_grad: float32 [2, 1024, 1024], P(None, 'tp', 'seq')
- ffn_gain_grad: float32 [2, 1024], P(None, 'tp')
- gate_grad: float32 [2, 1024, 4608], P(None, 'seq', 'tp')
- up_grad: float32 [2, 1024, 4608], P(None, 'seq', 'tp')
- down_grad: float32 [2, 4608, 1024], P(None, 'tp', 'seq')
All inputs are finite; a program needn't handle non-finite values.
Results may differ from a plain program's by a relative error of at most 0.022.
Values may be sent and summed in bfloat16 or wider, within the bound.
A program may use at most 256 MiB of HBM per device.

v0:
```python
import jax
import jax.numpy as jnp
from jax import lax
from jax.sharding import PartitionSpec as P

LAYERS = 2


EPS = 1e-05


def passed_along(block, axis, distance):
    devices = range(lax.axis_size(axis))
    route = [(i - distance, i) for i in devices if i - distance in devices]
    return lax.ppermute(block, axis, route)


def norm_rate(hidden):
    return lax.rsqrt(jnp.mean(hidden * hidden, axis=-1, keepdims=True) + EPS)


def norm_back(grad_in, gain, normed_val, rate):
    scaled = grad_in * gain
    return rate * (scaled - normed_val * jnp.mean(scaled * normed_val, axis=-1, keepdims=True))


def reduce_weights(grads):
    return (
        lax.psum_scatter(
            grads[0].astype(jnp.bfloat16), "seq", scatter_dimension=1, tiled=True
        ).astype(jnp.float32),
        lax.psum_scatter(
            grads[1].astype(jnp.bfloat16), "seq", scatter_dimension=2, tiled=True
        ).astype(jnp.float32),
        lax.psum_scatter(
            grads[2].astype(jnp.bfloat16), "seq", scatter_dimension=1, tiled=True
        ).astype(jnp.float32),
        lax.psum_scatter(
            grads[3].astype(jnp.bfloat16), "seq", scatter_dimension=1, tiled=True
        ).astype(jnp.float32),
        lax.psum_scatter(
            grads[4].astype(jnp.bfloat16), "seq", scatter_dimension=2, tiled=True
        ).astype(jnp.float32),
    )


def reduce_small(grads):
    return lax.psum((grads[0], grads[1], grads[2]), "seq")


def body(
    stream_in,
    norm_gain,
    in_proj,
    conv_taps,
    out_proj,
    ffn_gain,
    gate_proj,
    up_proj,
    down_proj,
    out_grad,
):
    f32 = jnp.float32
    bf16 = jnp.bfloat16
    width = in_proj.shape[-1]
    offset = lax.axis_index("tp") * width
    hidden = stream_in.astype(f32)
    kept = []
    for layer in range(LAYERS):
        gain_one = norm_gain[layer].astype(f32)
        gain_two = ffn_gain[layer].astype(f32)
        taps = conv_taps[layer].astype(f32)
        rate_one = norm_rate(hidden)
        normed_one = hidden * rate_one
        first = (normed_one * gain_one).astype(bf16)
        proj = jnp.einsum("msd,dkc->mskc", first, in_proj[layer], preferred_element_type=f32)
        bgate = proj[:, :, 0]
        cgate = proj[:, :, 1]
        xinput = proj[:, :, 2]
        mixed = (bgate * xinput).astype(bf16)
        prior = passed_along(mixed[:, -2:], "seq", 1)
        extended = jnp.concatenate([prior, mixed], axis=1).astype(f32)
        conved = (
            taps[0] * extended[:, :-2] + taps[1] * extended[:, 1:-1] + taps[2] * extended[:, 2:]
        )
        gated = (cgate * conved).astype(bf16)
        partial_out = jnp.einsum("msc,cd->msd", gated, out_proj[layer], preferred_element_type=f32)
        middle = hidden + lax.psum(partial_out, "tp")
        rate_two = norm_rate(middle)
        normed_two = middle * rate_two
        second = (normed_two * gain_two).astype(bf16)
        gate_val = jnp.einsum("msd,df->msf", second, gate_proj[layer], preferred_element_type=f32)
        up_val = jnp.einsum("msd,df->msf", second, up_proj[layer], preferred_element_type=f32)
        sigma = jax.nn.sigmoid(gate_val)
        silu_val = gate_val * sigma
        act = (silu_val * up_val).astype(bf16)
        partial_ffn = jnp.einsum("msf,fd->msd", act, down_proj[layer], preferred_element_type=f32)
        kept.append(
            (
                rate_one,
                normed_one,
                first,
                bgate,
                cgate,
                xinput,
                extended,
                conved,
                gated,
                rate_two,
                normed_two,
                second,
                gate_val,
                up_val,
                sigma,
                silu_val,
                act,
            )
        )
        hidden = middle + lax.psum(partial_ffn, "tp")
    grad_h = out_grad.astype(f32)
    collected = [None] * LAYERS
    for layer in reversed(range(LAYERS)):
        (
            rate_one,
            normed_one,
            first,
            bgate,
            cgate,
            xinput,
            extended,
            conved,
            gated,
            rate_two,
            normed_two,
            second,
            gate_val,
            up_val,
            sigma,
            silu_val,
            act,
        ) = kept[layer]
        gain_one = norm_gain[layer].astype(f32)
        gain_two = ffn_gain[layer].astype(f32)
        taps = conv_taps[layer].astype(f32)
        grad_f = grad_h.astype(bf16)
        grad_act = jnp.einsum("msd,fd->msf", grad_f, down_proj[layer], preferred_element_type=f32)
        down_g = jnp.einsum("msf,msd->fd", act, grad_f, preferred_element_type=f32)
        grad_gate = (grad_act * up_val * sigma * (1.0 + gate_val * (1.0 - sigma))).astype(bf16)
        grad_up = (grad_act * silu_val).astype(bf16)
        part_two = jnp.einsum(
            "msf,df->msd", grad_gate, gate_proj[layer], preferred_element_type=f32
        )
        part_two = part_two + jnp.einsum(
            "msf,df->msd", grad_up, up_proj[layer], preferred_element_type=f32
        )
        gate_g = jnp.einsum("msd,msf->df", second, grad_gate, preferred_element_type=f32)
        up_g = jnp.einsum("msd,msf->df", second, grad_up, preferred_element_type=f32)
        grad_two = lax.psum(part_two.astype(jnp.bfloat16), "tp").astype(jnp.float32)
        ffn_gain_g = jnp.sum(grad_two * normed_two, axis=(0, 1))
        grad_mid = grad_h + norm_back(grad_two, gain_two, normed_two, rate_two)
        grad_o = grad_mid.astype(bf16)
        grad_gated = jnp.einsum("msd,cd->msc", grad_o, out_proj[layer], preferred_element_type=f32)
        out_g = jnp.einsum("msc,msd->cd", gated, grad_o, preferred_element_type=f32)
        grad_conv = grad_gated * cgate
        grad_cgate = grad_gated * conved
        after = passed_along(grad_conv[:, :2], "seq", -1)
        grad_ext = jnp.concatenate([grad_conv, after], axis=1)
        grad_mixed = (
            taps[2] * grad_ext[:, :-2] + taps[1] * grad_ext[:, 1:-1] + taps[0] * grad_ext[:, 2:]
        )
        count = grad_conv.shape[1]
        conv_g = jnp.stack(
            [jnp.sum(grad_conv * extended[:, k : k + count], axis=(0, 1)) for k in range(3)], axis=0
        )
        grad_proj = jnp.stack([grad_mixed * xinput, grad_cgate, grad_mixed * bgate], axis=2).astype(
            bf16
        )
        part_one = jnp.einsum(
            "mskc,dkc->msd", grad_proj, in_proj[layer], preferred_element_type=f32
        )
        in_g = jnp.einsum("msd,mskc->dkc", first, grad_proj, preferred_element_type=f32)
        grad_one = lax.psum(part_one.astype(jnp.bfloat16), "tp").astype(jnp.float32)
        norm_gain_g = jnp.sum(grad_one * normed_one, axis=(0, 1))
        grad_h = grad_mid + norm_back(grad_one, gain_one, normed_one, rate_one)
        norm_piece = lax.dynamic_slice_in_dim(norm_gain_g, offset, width)
        ffn_piece = lax.dynamic_slice_in_dim(ffn_gain_g, offset, width)
        small = (norm_piece, conv_g, ffn_piece)
        large = (in_g, out_g, gate_g, up_g, down_g)
        collected[layer] = (small, large)
    norm_stack = jnp.stack([c[0][0] for c in collected], axis=0)
    conv_stack = jnp.stack([c[0][1] for c in collected], axis=0)
    ffn_stack = jnp.stack([c[0][2] for c in collected], axis=0)
    large_stack = tuple((jnp.stack([c[1][i] for c in collected], axis=0) for i in range(5)))
    large_stack = reduce_weights(large_stack)
    norm_stack, conv_stack, ffn_stack = reduce_small((norm_stack, conv_stack, ffn_stack))
    stream_out = hidden.astype(bf16)
    in_grad, out_grad_w, gate_grad, up_grad, down_grad = large_stack
    return (
        stream_out,
        grad_h,
        norm_stack,
        in_grad,
        conv_stack,
        out_grad_w,
        ffn_stack,
        gate_grad,
        up_grad,
        down_grad,
    )


def solution(mesh):
    in_specs = (
        P(None, "seq", None),
        P(),
        P(None, None, None, "tp"),
        P(None, None, "tp"),
        P(None, "tp", None),
        P(),
        P(None, None, "tp"),
        P(None, None, "tp"),
        P(None, "tp", None),
        P(None, "seq", None),
    )
    out_specs = (
        P(None, "seq", None),
        P(None, "seq", None),
        P(None, "tp"),
        P(None, "seq", None, "tp"),
        P(None, None, "tp"),
        P(None, "tp", "seq"),
        P(None, "tp"),
        P(None, "seq", "tp"),
        P(None, "seq", "tp"),
        P(None, "tp", "seq"),
    )
    return jax.shard_map(body, mesh=mesh, in_specs=in_specs, out_specs=out_specs, check_vma=False)
```

profile of v0, /device:TPU:0, one launch (start us, length us, event | category | flops | bytes accessed | tf_op | source)
XLA Modules:
  0.0 1165.2 jit_solution(9607039285124597385)
XLA Ops:
  26.1 87.0 %all-reduce.10.cloned.1.call-done = f32[4,256,1024]{2,1,0:T(8,128)} async-done(((f32[4,256,1024]{2,1,0:T(8,128)}), f32[4,256,1024]{2,1,0:T(8,128)}) %all-reduce.10.cloned.1.call-update) | async-done | bytes 4194320 | tf_op jit(solution)/shard_map/psum | solution.py:88
  118.0 6.0 fusion.59
  134.6 85.7 %all-reduce.12.cloned.1.call-done = f32[4,256,1024]{2,1,0:T(8,128)} async-done(((f32[4,256,1024]{2,1,0:T(8,128)}), f32[4,256,1024]{2,1,0:T(8,128)}) %all-reduce.12.cloned.1.call-update) | async-done | bytes 4194320 | tf_op jit(solution)/shard_map/psum | solution.py:119
  235.6 7.6 fusion.37
  243.2 79.0 %all-reduce.14.cloned.1.call-done = f32[4,256,1024]{2,1,0:T(8,128)} async-done(((f32[4,256,1024]{2,1,0:T(8,128)}), f32[4,256,1024]{2,1,0:T(8,128)}) %all-reduce.14.cloned.1.call-update) | async-done | bytes 4194320 | tf_op jit(solution)/shard_map/psum | solution.py:88
  328.3 6.1 fusion.43
  334.5 6.6 multiply_convert_fusion.3
  350.2 7.3 fusion.39
  357.6 44.0 %all-reduce.18.cloned.1.call-done = bf16[4,256,1024]{2,1,0:T(8,128)(2,1)} async-done(((bf16[4,256,1024]{2,1,0:T(8,128)(2,1)}), bf16[4,256,1024]{2,1,0:T(8,128)(2,1)}) %all-reduce.18.cloned.1.call-update) | async-done | bytes 2097168 | tf_op jit(solution)/shard_map/psum | solution.py:158
  406.1 83.4 %all-reduce.16.cloned.1.call-done = f32[4,256,1024]{2,1,0:T(8,128)} async-done(((f32[4,256,1024]{2,1,0:T(8,128)}), f32[4,256,1024]{2,1,0:T(8,128)}) %all-reduce.16.cloned.1.call-update) | async-done | bytes 4194320 | tf_op jit(solution)/shard_map/psum | solution.py:119
  489.5 6.7 fusion.23
  510.9 51.2 %all-reduce.20.cloned.1.call-done = bf16[4,256,1024]{2,1,0:T(8,128)(2,1)} async-done(((bf16[4,256,1024]{2,1,0:T(8,128)(2,1)}), bf16[4,256,1024]{2,1,0:T(8,128)(2,1)}) %all-reduce.20.cloned.1.call-update) | async-done | bytes 2097168 | tf_op jit(solution)/shard_map/psum | solution.py:182
  569.9 9.1 multiply_convert_fusion.1
  586.3 51.6 %all-reduce.22.cloned.1.call-done = bf16[4,256,1024]{2,1,0:T(8,128)(2,1)} async-done(((bf16[4,256,1024]{2,1,0:T(8,128)(2,1)}), bf16[4,256,1024]{2,1,0:T(8,128)(2,1)}) %all-reduce.22.cloned.1.call-update) | async-done | bytes 2097168 | tf_op jit(solution)/shard_map/psum | solution.py:158
  688.4 12.6 %copy.88 = bf16[2,1152,1024]{1,0,2:T(2,128)(2,1)} copy(bf16[2,1152,1024]{2,1,0:T(8,128)(2,1)} %pad_maximum_fusion.2) | data formatting | bytes 9437184
  701.0 5.4 copy.95
  706.5 5.4 fusion.34
  718.2 5.4 fusion.32
  733.3 35.8 %all-reduce = (f32[2,256]{1,0:T(2,128)}, f32[2,3,256]{2,1,0:T(4,128)S(1)}, f32[2,256]{1,0:T(2,128)}) all-reduce(f32[2,256]{1,0:T(2,128)S(1)} %pad_maximum_fusion.14, f32[2,3,256]{2,1,0:T(4,128)S(1)} %pad_maximum_fusion.13, f32[2,256]{1,0:T(2,128)S(1)} %pad_maximum_fusion.15), channel_id=1, replica_groups=mesh['seq'=8,'tp'=4] {'seq'}, use_global_device_ids=true, to_apply=%region_18.0 | all-reduce | flops 2560 | bytes 20480 | tf_op jit(solution)/shard_map/psum | solution.py:48
  774.4 6.6 reduce-scatter.16.cloned.1.call-done
  782.8 76.1 %reduce-scatter.10.cloned.1.call-done = bf16[2,128,3,256]{3,1,2,0:T(8,128)(2,1)} async-done(((bf16[2,1024,3,256]{3,1,2,0:T(8,128)(2,1)}), bf16[2,128,3,256]{3,1,2,0:T(8,128)(2,1)}) %reduce-scatter.10.cloned.1.call-update) | async-done | bytes 393232 | tf_op jit(solution)/shard_map/reduce_scatter | solution.py:29
  860.9 96.7 %reduce-scatter.18.cloned.1.call-done = bf16[128,2304]{1,0:T(8,128)(2,1)} async-done(((bf16[1024,2304]{1,0:T(8,128)(2,1)}), bf16[128,2304]{1,0:T(8,128)(2,1)}) %reduce-scatter.18.cloned.1.call-update) | async-done | bytes 589840
  961.3 95.5 %reduce-scatter.14.cloned.1.call-done = bf16[2,128,1152]{2,1,0:T(8,128)(2,1)} async-done(((bf16[2,1024,1152]{2,1,0:T(8,128)(2,1)}), bf16[2,128,1152]{2,1,0:T(8,128)(2,1)}) %reduce-scatter.14.cloned.1.call-update) | async-done | bytes 589840 | tf_op jit(solution)/shard_map/reduce_scatter | solution.py:38
  1058.9 97.1 %reduce-scatter.12.cloned.1.call-done = bf16[2,128,1152]{2,1,0:T(8,128)(2,1)} async-done(((bf16[2,1024,1152]{2,1,0:T(8,128)(2,1)}), bf16[2,128,1152]{2,1,0:T(8,128)(2,1)}) %reduce-scatter.12.cloned.1.call-update) | async-done | bytes 589840 | tf_op jit(solution)/shard_map/reduce_scatter | solution.py:35
  (294 shorter events, 181.6 us)
Async XLA Ops:
  7.2 105.9 %all-reduce.10.cloned.1.call-start = ((), (), s32[]{:S(2)}) async-start(), calls=%async_computation.5 | async-start | bytes 8388608 | tf_op jit(solution)/shard_map/psum | solution.py:88
  14.2 6.2 collective-permute-start
  25.4 87.7 %copy-start.8 = (bf16[4,256,1024]{2,1,0:T(8,128)(2,1)S(1)}, bf16[4,256,1024]{2,1,0:T(8,128)(2,1)}, u32[]{:S(2)}) copy-start(bf16[4,256,1024]{2,1,0:T(8,128)(2,1)} %param.10) | copy-start | bytes 6291460
  25.4 194.9 %all-reduce.12.cloned.1.call-start = ((), (), s32[]{:S(2)}) async-start(), calls=%async_computation.6 | async-start | bytes 8388608 | tf_op jit(solution)/shard_map/psum | solution.py:119
  118.0 12.1 %slice-start = ((s8[4718592]{0:T(1024)(128)(4,1)}), s8[4194304]{0:T(1024)(128)(4,1)S(1)}, s32[]{:S(2)}) async-start(s8[4718592]{0:T(1024)(128)(4,1)} %bitcast.337), calls=%async_computation.18 | async-start | bytes 8388608
  134.6 187.6 %all-reduce.14.cloned.1.call-start = ((), (), s32[]{:S(2)}) async-start(), calls=%async_computation.7 | async-start | bytes 8388608 | tf_op jit(solution)/shard_map/psum | solution.py:88
  226.7 4.7 collective-permute-start.1
  235.6 166.1 %all-reduce.18.cloned.1.call-start = ((), (), s32[]{:S(2)}) async-start(), calls=%async_computation.9 | async-start | bytes 4194304 | tf_op jit(solution)/shard_map/psum | solution.py:158
  328.3 12.7 %slice-start.6 = ((s8[4718592]{0:T(1024)(128)(4,1)}), s8[4194304]{0:T(1024)(128)(4,1)S(1)}, s32[]{:S(2)}) async-start(s8[4718592]{0:T(1024)(128)(4,1)} %bitcast.343), calls=%async_computation.24 | async-start | bytes 8388608
  349.9 139.5 %all-reduce.16.cloned.1.call-start = ((), (), s32[]{:S(2)}) async-start(), calls=%async_computation.8 | async-start | bytes 8388608 | tf_op jit(solution)/shard_map/psum | solution.py:119
  357.5 204.5 %all-reduce.20.cloned.1.call-start = ((), (), s32[]{:S(2)}) async-start(), calls=%async_computation.10 | async-start | bytes 4194304 | tf_op jit(solution)/shard_map/psum | solution.py:182
  500.0 5.8 collective-permute-start.2
  510.4 127.4 %all-reduce.22.cloned.1.call-start = ((), (), s32[]{:S(2)}) async-start(), calls=%async_computation.11 | async-start | bytes 4194304 | tf_op jit(solution)/shard_map/psum | solution.py:158
  566.8 12.2 %slice-start.8 = ((s8[4718592]{0:T(1024)(128)(4,1)}), s8[4194304]{0:T(1024)(128)(4,1)S(1)}, s32[]{:S(2)}) async-start(s8[4718592]{0:T(1024)(128)(4,1)} %bitcast.345), calls=%async_computation.26 | async-start | bytes 8388608
  566.8 15.2 %slice-start.12 = ((s8[4718592]{0:T(1024)(128)(4,1)}), s8[4194304]{0:T(1024)(128)(4,1)S(1)}, s32[]{:S(2)}) async-start(s8[4718592]{0:T(1024)(128)(4,1)} %bitcast.349), calls=%async_computation.30 | async-start | bytes 8388608
  569.8 9.2 copy-start.25
  569.8 12.1 %slice-start.13 = ((s8[4718592]{0:T(1024)(128)(4,1)}), s8[524288]{0:T(1024)(128)(4,1)S(1)}, s32[]{:S(2)}) async-start(s8[4718592]{0:T(1024)(128)(4,1)} %bitcast.349), calls=%async_computation.31 | async-start | bytes 1048576
  586.2 143.6 %all-reduce.24.cloned.1.call-start = ((), (), s32[]{:S(2)}) async-start(), calls=%async_computation.12 | async-start | bytes 4194304 | tf_op jit(solution)/shard_map/psum | solution.py:182
  651.5 5.8 collective-permute-start.3
  662.0 119.0 %reduce-scatter.16.cloned.1.call-start = ((), (), s32[]{:S(2)}) async-start(), calls=%async_computation.16 | async-start | bytes 1179648
  668.7 190.2 %reduce-scatter.10.cloned.1.call-start = ((), (), s32[]{:S(2)}) async-start(), calls=%async_computation.13 | async-start | bytes 3538944 | tf_op jit(solution)/shard_map/reduce_scatter | solution.py:29
  677.4 280.2 %reduce-scatter.18.cloned.1.call-start = ((), (), s32[]{:S(2)}) async-start(), calls=%async_computation.17 | async-start | bytes 5308416
  706.4 350.4 %reduce-scatter.14.cloned.1.call-start = ((), (), s32[]{:S(2)}) async-start(), calls=%async_computation.15 | async-start | bytes 5308416 | tf_op jit(solution)/shard_map/reduce_scatter | solution.py:38
  717.9 438.2 %reduce-scatter.12.cloned.1.call-start = ((), (), s32[]{:S(2)}) async-start(), calls=%async_computation.14 | async-start | bytes 5308416 | tf_op jit(solution)/shard_map/reduce_scatter | solution.py:35
  (74 other events, 332.0 us)
Sparse Core Ops, SparseCore 0:
  25.6 87.4 all-reduce.9
  134.7 85.6 all-reduce.11
  235.7 86.4 all-reduce.13
  350.1 51.5 all-reduce.17
  403.9 85.5 all-reduce.15
  510.5 51.4 all-reduce.19
  586.3 51.4 all-reduce.21
  662.1 51.4 all-reduce.23
  717.6 63.3 reduce-scatter.15
  784.9 73.9 reduce-scatter.9
  863.0 94.5 reduce-scatter.17
  961.6 95.1 reduce-scatter.13
  1060.9 95.1 reduce-scatter.11
where the time goes:
time: 1170 us
  waiting for transfers between devices  865 us (74%)
  matrix products  122 us (10%)
  other arithmetic  73 us (6%)
  local copies, waits for them, and re-layouts  40.1 us (3%)
  blocking collectives  35.8 us (3%)
  between operations  15.6 us (1%)
  starting transfers between devices  13.3 us (1%)
    psum x2, waiting for transfers between devices, body(): hidden = middle + lax.psum(partial_ffn, 'tp')  169 us
    psum x2, waiting for transfers between devices, body(): middle = hidden + lax.psum(partial_out, 'tp')  166 us
    unnamed x15, waiting for transfers between devices  104 us
    reduce_scatter x1, waiting for transfers between devices, reduce_weights(): lax.psum_scatter(grads[2].astype(jnp.bfloat16), 'seq', scatter_dimension=...  97.1 us
    psum x2, waiting for transfers between devices, body(): grad_two = lax.psum(part_two.astype(jnp.bfloat16), 'tp').astype(jnp.float32)  95.6 us
    reduce_scatter x1, waiting for transfers between devices, reduce_weights(): lax.psum_scatter(grads[3].astype(jnp.bfloat16), 'seq', scatter_dimension=...  95.5 us
    reduce_scatter x1, waiting for transfers between devices, reduce_weights(): lax.psum_scatter(grads[0].astype(jnp.bfloat16), 'seq', scatter_dimension=...  76.1 us
    psum x2, waiting for transfers between devices, body(): grad_one = lax.psum(part_one.astype(jnp.bfloat16), 'tp').astype(jnp.float32)  51.2 us
  transfers between devices with their start and end apart: 17, of which 16 were waited for; matrix products, arithmetic and copies ran while one was open for 9% of the time, Pallas kernels for 0%

commit v1 on v0

--- a/solution.py
+++ b/solution.py
@@ -1,6 +1,10 @@
+import functools
+
 import jax
 import jax.numpy as jnp
 from jax import lax
+from jax.experimental import pallas as pl
+from jax.experimental.pallas import tpu as pltpu
 from jax.sharding import PartitionSpec as P
 
 LAYERS = 2
@@ -209,6 +213,621 @@
     )
 
 
+VMEM_BYTES = 62 * 2**20
+MESH = pl.DeviceIdType.MESH
+f32 = jnp.float32
+bf16 = jnp.bfloat16
+NN = (((1,), (0,)), ((), ()))
+NT = (((1,), (1,)), ((), ()))
+ORDERS = ((0, 1, 2), (1, 2, 0))
+SLOTS = 4
+N1, N2, DF, DO = range(4)
+
+
+def mm(lhs, rhs, dims=NN):
+    return lax.dot_general(lhs, rhs, dims, preferred_element_type=f32)
+
+
+def fused(
+    dims,
+    stream_in, norm_gain, win, taps, wout, ffn_gain, wgate, wup, wdown, out_grad,
+    out_stream, out_sgrad, out_units, out_small,
+    L, R, WIN, WOUT, WG, WU, WD, H, RATE, PB, PR, XR,
+    GA, GB, RA0, RA1, RA2, RB0, RB1, RB2, RT, FO,
+    EXT, DYE, CF, HALO, DHALO, GAIN, TAPS, GACC, CACC, SMR,
+    load_sem, ps, pr, xs, xr, ags, agr, hs, hr, rss, rsr, fos, oss, sms, smr,
+):
+    M, TOK, D, C, F, U = dims
+    half = TOK // 2
+    CS, CA, CB, CP, CZ = 0, F, 2 * F, 3 * F, 3 * F + 3 * C
+    UNITS = 2 * (-(-(CZ + C) // U))
+    PER = UNITS // 2
+    rows_of = (GA.shape[2], GB.shape[2])
+    seq = lax.axis_index("seq")
+    tp = lax.axis_index("tp")
+    n = lax.axis_size("seq")
+    core = lax.rem(tp, 2)
+    xi = lax.div(tp, 2)
+    sib = {"seq": seq, "tp": tp + 1 - 2 * core}
+    xpart = {"seq": seq, "tp": tp + 2 - 4 * xi}
+    bits = [lax.rem(lax.div(seq, 1 << k), 2) for k in range(3)]
+    parts = [{"seq": seq + (1 << k) - 2 * (1 << k) * bits[k], "tp": tp} for k in range(3)]
+    nxt = {"seq": lax.rem(seq + 1, n), "tp": tp}
+    prv = {"seq": lax.rem(seq + n - 1, n), "tp": tp}
+    mine = pl.ds(pl.multiple_of(core * half, half), half)
+    theirs = pl.ds(pl.multiple_of((1 - core) * half, half), half)
+
+    def remote(src, dst, ssem, rsem, dev):
+        return pltpu.make_async_remote_copy(
+            src_ref=src, dst_ref=dst, send_sem=ssem, recv_sem=rsem, device_id=dev, device_id_type=MESH
+        )
+
+    def load_stream(m):
+        return pltpu.make_async_copy(stream_in.at[m], L.at[0, N1, m], load_sem.at[m])
+
+    def load_conv(l):
+        b = 4 + 4 * l
+        return [
+            pltpu.make_async_copy(win.at[l, k], WIN.at[l, :, pl.ds(k * C, C)], load_sem.at[b + k])
+            for k in range(3)
+        ] + [pltpu.make_async_copy(wout.at[l], WOUT.at[l], load_sem.at[b + 3])]
+
+    def load_ffn(l):
+        return [
+            pltpu.make_async_copy(s.at[l], d, load_sem.at[12 + i])
+            for i, (s, d) in enumerate(((wgate, WG), (wup, WU), (wdown, WD)))
+        ]
+
+    load_og = pltpu.make_async_copy(out_grad, L.at[1, DF], load_sem.at[15])
+    for m in range(M):
+        load_stream(m).start()
+    for cp in load_conv(0) + load_ffn(0) + load_conv(1) + [load_og]:
+        cp.start()
+
+    barrier = pltpu.get_barrier_semaphore()
+    others = [sib, xpart, nxt, prv] + parts
+    for dev in others:
+        pl.semaphore_signal(barrier, inc=1, device_id=dev, device_id_type=MESH)
+
+    GAIN[0] = norm_gain[...].astype(f32)
+    GAIN[1] = ffn_gain[...].astype(f32)
+    GAIN[2] = 1.0 / norm_gain[...].astype(f32)
+    GAIN[3] = 1.0 / ffn_gain[...].astype(f32)
+    TAPS[...] = taps[...].astype(f32)
+    GACC[...] = jnp.zeros_like(GACC)
+    CACC[...] = jnp.zeros_like(CACC)
+
+    pl.semaphore_wait(barrier, len(others))
+
+    def pcopy(m):
+        return remote(PB.at[m, theirs], PR.at[m], ps.at[m], pr.at[m], sib)
+
+    def xcopy(m):
+        return remote(PB.at[m, mine], XR.at[m], xs.at[m], xr.at[m], xpart)
+
+    def mid(m):
+        pcopy(m).wait()
+
+        def chunk(i, _):
+            off = pl.multiple_of(i * 32, 32)
+            rows = pl.ds(pl.multiple_of(core * half + off, 32), 32)
+            got = PR[m, pl.ds(off, 32)].astype(f32) + PB[m, rows].astype(f32)
+            PB[m, rows] = got.astype(bf16)
+            return 0
+
+        lax.fori_loop(0, half // 32, chunk, 0)
+        xcopy(m).start()
+
+    def agcopy(l, kind, m):
+        ref = L.at[l, kind, m, mine]
+        return remote(ref, ref, ags.at[m], agr.at[m], sib)
+
+    def rows_loop(m, body):
+        def chunk(i, _):
+            off = pl.multiple_of(i * 32, 32)
+            rows = pl.ds(pl.multiple_of(core * half + off, 32), 32)
+            total = PB[m, rows].astype(f32) + XR[m, pl.ds(off, 32)].astype(f32)
+            body(pl.ds(off, 32), rows, total)
+            return 0
+
+        lax.fori_loop(0, half // 32, chunk, 0)
+
+    def rate_of(val):
+        return lax.rsqrt(jnp.mean(val * val, axis=-1, keepdims=True) + EPS)
+
+    def finish_norm(l, which, kind, m):
+        xcopy(m).wait()
+        gain = GAIN[which, l : l + 1, :]
+
+        def body(loc, rows, total):
+            hid = H[m, loc] + total
+            H[m, loc] = hid
+            rate = rate_of(hid)
+            RATE[l, which, m, loc] = rate
+            L[l, kind, m, rows] = (hid * rate * gain).astype(bf16)
+
+        rows_loop(m, body)
+        agcopy(l, kind, m).start()
+
+    def stream_copies(m):
+        ref = PB.at[m, mine]
+        return (
+            pltpu.make_async_copy(ref, out_stream.at[m, mine], oss.at[m]),
+            remote(ref, out_stream.at[m, mine], ags.at[m], agr.at[m], sib),
+        )
+
+    def finish_stream(m):
+        xcopy(m).wait()
+
+        def body(loc, rows, total):
+            PB[m, rows] = (H[m, loc] + total).astype(bf16)
+
+        rows_loop(m, body)
+        for cp in stream_copies(m):
+            cp.start()
+
+    def norm_back(l, which, kind, m, emit):
+        xcopy(m).wait()
+        gain = GAIN[which, l : l + 1, :]
+        inv = GAIN[2 + which, l : l + 1, :]
+
+        def body(loc, rows, total):
+            nrm = L[l, kind, m, rows].astype(f32) * inv
+            prod = total * nrm
+            GACC[2 * which + l] += prod[0:8] + prod[8:16] + prod[16:24] + prod[24:32]
+            mean = jnp.mean(prod * gain, axis=-1, keepdims=True)
+            emit(loc, rows, RATE[l, which, m, loc] * (total * gain - nrm * mean))
+
+        rows_loop(m, body)
+
+    def finish_dn2(l, m):
+        def emit(loc, rows, delta):
+            prev = L[1, DF, m, rows].astype(f32) if l == 1 else H[m, loc]
+            new = prev + delta
+            H[m, loc] = new
+            L[l, DO, m, rows] = new.astype(bf16)
+
+        norm_back(l, 1, N2, m, emit)
+        agcopy(l, DO, m).start()
+
+    def finish_dn1(l, m):
+        def emit(loc, rows, delta):
+            new = H[m, loc] + delta
+            H[m, loc] = new
+            if l == 1:
+                L[0, DF, m, rows] = new.astype(bf16)
+
+        norm_back(l, 0, N1, m, emit)
+        if l == 1:
+            agcopy(0, DF, m).start()
+        else:
+            for cp in grad_copies(m):
+                cp.start()
+
+    def grad_copies(m):
+        return (
+            pltpu.make_async_copy(H.at[m], out_sgrad.at[m, mine], oss.at[m]),
+            remote(H.at[m], out_sgrad.at[m, mine], ags.at[m], agr.at[m], sib),
+        )
+
+    def put_partial(m, tile):
+        def step(j, _):
+            cols = pl.ds(pl.multiple_of(j * 256, 256), 256)
+            PB[m, :, cols] = tile(cols).astype(bf16)
+            return 0
+
+        lax.fori_loop(0, D // 256, step, 0)
+        pcopy(m).start()
+
+    def hcopy(l, m):
+        return remote(EXT.at[pl.ds(TOK, 8)], HALO.at[l, m], hs, hr.at[0, l, m], nxt)
+
+    def dhcopy(l, m):
+        return remote(DYE.at[pl.ds(0, 8)], DHALO.at[l, m], hs, hr.at[1, l, m], prv)
+
+    def tap(l, k):
+        return TAPS[k, l : l + 1, :]
+
+    def conv_now(l, m):
+        EXT[0:8] = jnp.where(seq == 0, 0.0, HALO[l, m])
+        return (
+            tap(l, 0) * EXT[6 : 6 + TOK] + tap(l, 1) * EXT[7 : 7 + TOK] + tap(l, 2) * EXT[8 : 8 + TOK]
+        )
+
+    def conv_fwd_a(l, m):
+        if l == 0:
+            load_stream(m).wait()
+            gain = GAIN[0, 0:1, :]
+            hid = L[0, N1, m, mine].astype(f32)
+            H[m] = hid
+            RATE[0, 0, m] = rate_of(hid)
+
+            def chunk(i, _):
+                rows = pl.ds(pl.multiple_of(i * 32, 32), 32)
+                val = L[0, N1, m, rows].astype(f32)
+                L[0, N1, m, rows] = (val * rate_of(val) * gain).astype(bf16)
+                return 0
+
+            lax.fori_loop(0, TOK // 32, chunk, 0)
+        else:
+            agcopy(1, N1, m).wait()
+        first = L[l, N1, m]
+        bgate = mm(first, WIN[l, :, 0:C])
+        R[l, m, :, CP : CP + C] = bgate.astype(bf16)
+        xin = mm(first, WIN[l, :, 2 * C : 3 * C])
+        R[l, m, :, CP + 2 * C : CP + 3 * C] = xin.astype(bf16)
+        EXT[8 : 8 + TOK] = (bgate * xin).astype(bf16).astype(f32)
+        hcopy(l, m).start()
+        cgate = mm(first, WIN[l, :, C : 2 * C])
+        R[l, m, :, CP + C : CP + 2 * C] = cgate.astype(bf16)
+        CF[...] = cgate
+
+    def conv_fwd_b(l, m):
+        hcopy(l, m).wait()
+        R[l, m, :, CZ : CZ + C] = (CF[...] * conv_now(l, m)).astype(bf16)
+        gated = R[l, m, :, CZ : CZ + C]
+        put_partial(m, lambda cols: mm(gated, WOUT[l, :, cols]))
+
+    def ffn_tiles(body):
+        def step(t, _):
+            body(pl.multiple_of(t * U, 128))
+            return 0
+
+        lax.fori_loop(0, F // U, step, 0)
+
+    def ffn_fwd(l, m):
+        agcopy(l, N2, m).wait()
+        second = L[l, N2, m]
+
+        def body(off):
+            cols = pl.ds(off, U)
+            a = mm(second, WG[:, cols])
+            b = mm(second, WU[:, cols])
+            sig = jax.nn.sigmoid(a)
+            silu = a * sig
+            R[l, m, :, pl.ds(CS + off, U)] = (silu * b).astype(bf16)
+            if l == 0:
+                R[l, m, :, pl.ds(CA + off, U)] = a.astype(bf16)
+                R[l, m, :, pl.ds(CB + off, U)] = b.astype(bf16)
+            else:
+                ds = mm(L[l, DF, m], WD[pl.ds(off, U), :], NT)
+                R[l, m, :, pl.ds(CA + off, U)] = (ds * b * sig * (1.0 + a * (1.0 - sig))).astype(bf16)
+                R[l, m, :, pl.ds(CB + off, U)] = (ds * silu).astype(bf16)
+
+        ffn_tiles(body)
+        act = R[l, m, :, CS : CS + F]
+        put_partial(m, lambda cols: mm(act, WD[:, cols]))
+
+    def ffn_bwd(l, m):
+        if l == 0:
+            agcopy(0, DF, m).wait()
+
+            def body(off):
+                a = R[l, m, :, pl.ds(CA + off, U)].astype(f32)
+                b = R[l, m, :, pl.ds(CB + off, U)].astype(f32)
+                sig = jax.nn.sigmoid(a)
+                ds = mm(L[l, DF, m], WD[pl.ds(off, U), :], NT)
+                R[l, m, :, pl.ds(CA + off, U)] = (ds * b * sig * (1.0 + a * (1.0 - sig))).astype(bf16)
+                R[l, m, :, pl.ds(CB + off, U)] = (ds * a * sig).astype(bf16)
+
+            ffn_tiles(body)
+        else:
+            for cp in stream_copies(m):
+                cp.wait()
+        da = R[l, m, :, CA : CA + F]
+        db = R[l, m, :, CB : CB + F]
+        put_partial(m, lambda cols: mm(da, WG[cols, :], NT) + mm(db, WU[cols, :], NT))
+
+    def conv_bwd_a(l, m):
+        agcopy(l, DO, m).wait()
+        dz = mm(L[l, DO, m], WOUT[l], NT)
+        bgate = R[l, m, :, CP : CP + C].astype(f32)
+        xin = R[l, m, :, CP + 2 * C : CP + 3 * C].astype(f32)
+        EXT[8 : 8 + TOK] = (bgate * xin).astype(bf16).astype(f32)
+        dy = dz * R[l, m, :, CP + C : CP + 2 * C].astype(f32)
+        DYE[0:TOK] = dy
+        dhcopy(l, m).start()
+        R[l, m, :, CP + C : CP + 2 * C] = (dz * conv_now(l, m)).astype(bf16)
+        for k in range(3):
+            prod = dy * EXT[6 + k : 6 + k + TOK]
+            CACC[l, k] += jnp.sum(prod.reshape(TOK // 8, 8, C), axis=0)
+
+    def conv_bwd_b(l, m):
+        dhcopy(l, m).wait()
+        DYE[TOK : TOK + 8] = jnp.where(seq == n - 1, 0.0, DHALO[l, m])
+        dbx = tap(l, 2) * DYE[0:TOK] + tap(l, 1) * DYE[1 : 1 + TOK] + tap(l, 0) * DYE[2 : 2 + TOK]
+        bgate = R[l, m, :, CP : CP + C].astype(f32)
+        xin = R[l, m, :, CP + 2 * C : CP + 3 * C].astype(f32)
+        R[l, m, :, CP : CP + C] = (dbx * xin).astype(bf16)
+        R[l, m, :, CP + 2 * C : CP + 3 * C] = (dbx * bgate).astype(bf16)
+        dp = R[l, m, :, CP : CP + 3 * C]
+        put_partial(m, lambda cols: mm(dp, WIN[l, cols, :], NT))
+
+    lanes = ((GA, (RA0, RA1, RA2)), (GB, (RB0, RB1, RB2)))
+
+    def keep(lane, step):
+        b = [bits[o] for o in ORDERS[lane]]
+        return [b[0] * 4, b[0] * 4 + b[1] * 2, b[0] * 4 + b[1] * 2 + b[2]][step]
+
+    def rs_copy(lane, step, t):
+        G, recv = lanes[lane]
+        slot = lax.rem(t, SLOTS)
+        size = 4 >> step
+        o = ORDERS[lane][step]
+        off = keep(lane, step) + size - 2 * size * bits[o]
+        return remote(
+            G.at[slot, pl.ds(off, size)], recv[step].at[slot],
+            rss.at[lane, step, slot], rsr.at[lane, step, slot], parts[o],
+        )
+
+    def rs_gen(t):
+        l = 1 - lax.div(t, PER)
+        v = lax.rem(t, PER)
+        fu = F // U
+        kind = jnp.where(v < fu, DF, jnp.where(v < 3 * fu, N2, jnp.where(v < PER - 1, N1, DO)))
+        slot = lax.rem(t, SLOTS)
+        cols = pl.ds(pl.multiple_of(v * U, 128), U)
+        for m in range(M):
+            RT[:, m * TOK : (m + 1) * TOK] = R[l, m, :, cols].T
+
+        def step(j, _):
+            src = L[l, kind, :, :, pl.ds(pl.multiple_of(j * 256, 256), 256)].reshape(M * TOK, 256)
+            res = mm(RT[...], src).astype(bf16)
+            hi, lo = lax.div(j, 2), lax.rem(j, 2)
+            cut = rows_of[0]
+            for y in range(2):
+                block = res[:, y * 128 : (y + 1) * 128]
+                GA[slot, y * 4 + lo * 2 + hi] = block[:cut]
+                GB[slot, lo * 4 + hi * 2 + y] = block[cut:]
+            return 0
+
+        lax.fori_loop(0, D // 256, step, 0)
+        for lane in range(2):
+            rs_copy(lane, 0, t).start()
+
+    def rs_add(step, t):
+        slot = lax.rem(t, SLOTS)
+        for lane in range(2):
+            G, recv = lanes[lane]
+            rs_copy(lane, step, t).wait()
+            base = keep(lane, step)
+
+            def add(i, _):
+                G[slot, base + i] = (
+                    G[slot, base + i].astype(f32) + recv[step][slot, i].astype(f32)
+                ).astype(bf16)
+                return 0
+
+            lax.fori_loop(0, 4 >> step, add, 0)
+            rs_copy(lane, step + 1, t).start()
+
+    def unit_copy(t):
+        l = 1 - lax.div(t, PER)
+        v = lax.rem(t, PER)
+        s = lax.rem(t, 2)
+        return pltpu.make_async_copy(
+            FO.at[s], out_units.at[l, pl.ds(pl.multiple_of(v * U, 128), U)], fos.at[s]
+        )
+
+    def rs_last(t):
+        slot = lax.rem(t, SLOTS)
+        s = lax.rem(t, 2)
+        for lane in range(2):
+            rs_copy(lane, 2, t).wait()
+
+        @pl.when(t >= 2)
+        def _():
+            unit_copy(t - 2).wait()
+
+        cut = rows_of[0]
+        FO[s, 0:cut] = GA[slot, keep(0, 2)].astype(f32) + RA2[slot, 0].astype(f32)
+        FO[s, cut:U] = GB[slot, keep(1, 2)].astype(f32) + RB2[slot, 0].astype(f32)
+        unit_copy(t).start()
+
+    def tick(t):
+        static = isinstance(t, int)
+
+        def at(cond, fn, arg):
+            if static:
+                if cond(t):
+                    fn(jnp.int32(arg))
+            else:
+                pl.when(cond(t))(lambda: fn(arg))
+
+        at(lambda q: q < UNITS, rs_gen, t)
+        at(lambda q: (q >= 1) & (q < UNITS + 1), functools.partial(rs_add, 0), t - 1)
+        at(lambda q: (q >= 2) & (q < UNITS + 2), functools.partial(rs_add, 1), t - 2)
+        at(lambda q: (q >= 3) & (q < UNITS + 3), rs_last, t - 3)
+
+    finishers = [
+        lambda m: finish_norm(0, 1, N2, m),
+        lambda m: finish_norm(1, 0, N1, m),
+        lambda m: finish_norm(1, 1, N2, m),
+        finish_stream,
+        lambda m: finish_dn2(1, m),
+        lambda m: finish_dn1(1, m),
+        lambda m: finish_dn2(0, m),
+        lambda m: finish_dn1(0, m),
+    ]
+
+    def behind(p, m):
+        @pl.when((m > 0) | (p > 0))
+        def _():
+            mid(lax.rem(m + M - 1, M))
+
+        if p > 0:
+            @pl.when(m < 2)
+            def _():
+                finishers[p - 1](m + M - 2)
+
+        @pl.when(m >= 2)
+        def _():
+            finishers[p](m - 2)
+
+    def phase(p, first, second, tick_base=None):
+        def step(m, _):
+            first(m)
+            if second is None:
+                behind(p, m)
+                if tick_base is not None:
+                    tick(tick_base + m)
+            else:
+                if tick_base is not None:
+                    tick(tick_base + m)
+                behind(p, m)
+                second(m)
+            return 0
+
+        lax.fori_loop(0, M, step, 0)
+
+    def arrived(copies):
+        for cp in copies:
+            cp.wait()
+
+    arrived(load_conv(0))
+    phase(0, lambda m: conv_fwd_a(0, m), lambda m: conv_fwd_b(0, m))
+    arrived(load_ffn(0))
+    phase(1, lambda m: ffn_fwd(0, m), None)
+    for cp in load_ffn(1):
+        cp.start()
+    arrived(load_conv(1))
+    phase(2, lambda m: conv_fwd_a(1, m), lambda m: conv_fwd_b(1, m))
+    arrived(load_ffn(1) + [load_og])
+    phase(3, lambda m: ffn_fwd(1, m), None)
+    phase(4, lambda m: ffn_bwd(1, m), None, 0)
+    for cp in load_ffn(0):
+        cp.start()
+    phase(5, lambda m: conv_bwd_a(1, m), lambda m: conv_bwd_b(1, m), M)
+    arrived(load_ffn(0))
+    phase(6, lambda m: ffn_bwd(0, m), None, 2 * M)
+    phase(7, lambda m: conv_bwd_a(0, m), lambda m: conv_bwd_b(0, m), 3 * M)
+    mid(M - 1)
+    finishers[7](M - 2)
+    tick(4 * M)
+    finishers[7](M - 1)
+
+    for i in range(4):
+        out_small[i : i + 1] = jnp.sum(GACC[i], axis=0, keepdims=True)
+    out_small[4:8] = jnp.zeros((4, D), f32)
+    for l in range(2):
+        for k in range(3):
+            out_small[4 + l : 5 + l, k * C : (k + 1) * C] = jnp.sum(CACC[l, k], axis=0, keepdims=True)
+
+    def small(i):
+        return remote(out_small, SMR.at[i], sms.at[i], smr.at[i], [sib, *parts][i])
+
+    small(0).start()
+    t = 4 * M + 1
+    for i in range(4):
+        tick(t)
+        t += 1
+        small(i).wait()
+        if i == 0:
+            out_small[0:4] += SMR[0, 0:4]
+        else:
+            out_small[...] += SMR[i]
+        if i < 3:
+            small(i + 1).start()
+    while t < UNITS + 3:
+        tick(t)
+        t += 1
+    for q in (UNITS - 2, UNITS - 1):
+        unit_copy(jnp.int32(q)).wait()
+    for m in range(M):
+        for cp in grad_copies(m):
+            cp.wait()
+
+
+def fused_call(stream_in, norm_gain, win, taps, wout, ffn_gain, wgate, wup, wdown, out_grad):
+    M, TOK, D = stream_in.shape
+    C, F = wout.shape[1], wgate.shape[2]
+    U = 384
+    per = -(-(3 * F + 4 * C) // U)
+    rb = U // 6
+    ra = U - rb
+    half = TOK // 2
+    vm = pltpu.VMEM
+    dma = pltpu.SemaphoreType.DMA
+    S = SLOTS
+    anys = pl.BlockSpec(memory_space=pl.ANY)
+    vmem = pl.BlockSpec(memory_space=pltpu.VMEM)
+    return pl.pallas_call(
+        functools.partial(fused, (M, TOK, D, C, F, U)),
+        out_shape=[
+            jax.ShapeDtypeStruct((M, TOK, D), bf16),
+            jax.ShapeDtypeStruct((M, TOK, D), f32),
+            jax.ShapeDtypeStruct((LAYERS, per * U, 128), f32),
+            jax.ShapeDtypeStruct((8, D), f32),
+        ],
+        in_specs=[anys, vmem, anys, vmem, anys, vmem, anys, anys, anys, anys],
+        out_specs=[anys, anys, anys, vmem],
+        scratch_shapes=[
+            vm((LAYERS, 4, M, TOK, D), bf16),
+            vm((LAYERS, M, TOK, per * U), bf16),
+            vm((LAYERS, D, 3 * C), bf16),
+            vm((LAYERS, C, D), bf16),
+            vm((D, F), bf16),
+            vm((D, F), bf16),
+            vm((F, D), bf16),
+            vm((M, half, D), f32),
+            vm((LAYERS, 2, M, half, 1), f32),
+            vm((M, TOK, D), bf16),
+            vm((M, half, D), bf16),
+            vm((M, half, D), bf16),
+            vm((S, 8, ra, 128), bf16),
+            vm((S, 8, rb, 128), bf16),
+            vm((S, 4, ra, 128), bf16),
+            vm((S, 2, ra, 128), bf16),
+            vm((S, 1, ra, 128), bf16),
+            vm((S, 4, rb, 128), bf16),
+            vm((S, 2, rb, 128), bf16),
+            vm((S, 1, rb, 128), bf16),
+            vm((U, M * TOK), bf16),
+            vm((2, U, 128), f32),
+            vm((TOK + 8, C), f32),
+            vm((TOK + 8, C), f32),
+            vm((TOK, C), f32),
+            vm((LAYERS, M, 8, C), f32),
+            vm((LAYERS, M, 8, C), f32),
+            vm((4, LAYERS, D), f32),
+            vm((3, LAYERS, C), f32),
+            vm((4, 8, D), f32),
+            vm((LAYERS, 3, 8, C), f32),
+            vm((4, 8, D), f32),
+            dma((16,)),
+            dma((M,)), dma((M,)), dma((M,)), dma((M,)), dma((M,)), dma((M,)),
+            dma, dma((2, LAYERS, M)),
+            dma((2, 3, S)), dma((2, 3, S)),
+            dma((2,)), dma((M,)), dma((4,)), dma((4,)),
+        ],
+        name="fused",
+        compiler_params=pltpu.CompilerParams(
+            collective_id=0, has_side_effects=True, vmem_limit_bytes=VMEM_BYTES
+        ),
+    )(stream_in, norm_gain, win, taps, wout, ffn_gain, wgate, wup, wdown, out_grad)
+
+
+def body_fused(
+    stream_in, norm_gain, in_proj, conv_taps, out_proj, ffn_gain, gate_proj, up_proj, down_proj, out_grad
+):
+    C, F = out_proj.shape[1], gate_proj.shape[2]
+    D = stream_in.shape[2]
+    out_stream, out_sgrad, units, small = fused_call(
+        stream_in, norm_gain, jnp.transpose(in_proj, (0, 2, 1, 3)), jnp.transpose(conv_taps, (1, 0, 2)),
+        out_proj, ffn_gain, gate_proj, up_proj, down_proj, out_grad,
+    )
+    offset = lax.axis_index("tp") * C
+    norm_g = lax.dynamic_slice_in_dim(small[0:2], offset, C, axis=1)
+    ffn_g = lax.dynamic_slice_in_dim(small[2:4], offset, C, axis=1)
+    conv_g = small[4:6, : 3 * C].reshape(LAYERS, 3, C)
+    down_g = units[:, :F]
+    gate_g = jnp.swapaxes(units[:, F : 2 * F], 1, 2)
+    up_g = jnp.swapaxes(units[:, 2 * F : 3 * F], 1, 2)
+    in_g = units[:, 3 * F : 3 * F + 3 * C].reshape(LAYERS, 3, C, 128).transpose(0, 3, 1, 2)
+    out_g = units[:, 3 * F + 3 * C : 3 * F + 4 * C]
+    return (out_stream, out_sgrad, norm_g, in_g, conv_g, out_g, ffn_g, gate_g, up_g, down_g)
+
+
 def solution(mesh):
     in_specs = (
         P(None, "seq", None),
@@ -234,4 +853,5 @@
         P(None, "seq", "tp"),
         P(None, "tp", "seq"),
     )
-    return jax.shard_map(body, mesh=mesh, in_specs=in_specs, out_specs=out_specs, check_vma=False)
+    chosen = body_fused if (mesh.shape["seq"], mesh.shape["tp"]) == (8, 4) else body
+    return jax.shard_map(chosen, mesh=mesh, in_specs=in_specs, out_specs=out_specs, check_vma=False)

time: 1170 us -> 325 us (0.28)
  waiting for transfers between devices: 865 us -> 0 us
  Pallas kernels: 0 us -> 305 us
  matrix products: 122 us -> 0 us
  other arithmetic: 73 us -> 0 us
  blocking collectives: 35.8 us -> 0 us
  local copies, waits for them, and re-layouts: 40.1 us -> 18.3 us
  between operations: 15.6 us -> 0.67 us
  starting transfers between devices: 13.3 us -> 0 us
    psum x8 -> x0, waiting for transfers between devices: 482 us -> none  [the longest x2 169 us: body(): hidden = middle + lax.psum(partial_ffn, 'tp')]
    pallas_call x0 -> x1, Pallas kernels: none -> 305 us  [fused_call(): pl.pallas_call(functools.partial(fused, (M, TOK, D, C, F, U)), out_shape=...]
    reduce_scatter x3 -> x0, waiting for transfers between devices: 269 us -> none  [the longest x1 97.1 us: reduce_weights(): lax.psum_scatter(grads[2].astype(jnp.bfloat16), 'seq', scatter_dimension=...]
    dot_general x30 -> x0, matrix products: 122 us -> none  [the longest x2 16.7 us: body(): jnp.einsum('msd,fd->msf', grad_f, down_proj[layer], preferred_element_typ...]
    unnamed x15 -> x0, waiting for transfers between devices: 104 us -> none
    psum x1 -> x0, blocking collectives: 35.8 us -> none  [reduce_small(): return lax.psum((grads[0], grads[1], grads[2]), 'seq')]
    unnamed x171 -> x8, local copies, waits for them, and re-layouts: 39.7 us -> 8.35 us
    reduce_sum x10 -> x0, other arithmetic: 30.8 us -> none  [the longest x4 13 us: norm_rate(): return lax.rsqrt(jnp.mean(hidden * hidden, axis=-1, keepdims=True) + EPS)]
  transfers between devices with their start and end apart: 17 -> 0, of which waited for: 16 -> 0; matrix products, arithmetic and copies ran while one was open for 9% -> 0% of each run, Pallas kernels for 0% -> 0%
where the time goes in v1:
time: 325 us; the launch traced here: 324 us
  Pallas kernels  305 us (94%)
  local copies, waits for them, and re-layouts  18.3 us (6%)
    pallas_call x1, Pallas kernels, fused_call(): pl.pallas_call(functools.partial(fused, (M, TOK, D, C, F, U)), out_shape=...  305 us
    unnamed x8, local copies, waits for them, and re-layouts  8.35 us

profile of v1, /device:TPU:0, one launch (start us, length us, event | category | flops | bytes accessed | tf_op | source)
XLA Modules:
  0.0 324.1 jit_solution(7590827040876772785)
XLA Ops:
  0.7 305.1 %fused.1 = (bf16[4,256,1024]{2,1,0:T(8,128)(2,1)}, f32[4,256,1024]{2,1,0:T(8,128)}, f32[2,4608,128]{2,1,0:T(8,128)}, f32[8,1024]{1,0:T(8,128)}) custom-call(bf16[4,256,1024]{2,1,0:T(8,128)(2,1)} %stream_in.1, bf16[2,1024]{1,0:T(2,128)(2,1)} %norm_gain.1, bf16[2,3,1024,256]{3,2,1,0:T(8,128)(2,1)} %bitcast.10, bf16[3,2,256]{2,1,0:T(2,128)(2,1)} %bitcast.13, ...), custom_call_target="tpu_custom_call" | custom-call | tf_op jit(solution)/shard_map/fused/pallas_call | solution.py:754
  305.7 1.3 slice.26
  307.0 0.8 fusion.1
  307.9 0.6 constant_dynamic-slice_fusion
  308.5 1.7 slice.27
  310.1 1.2 slice.25
  311.3 3.2 fusion
  314.6 1.1 copy.24
  315.7 1.4 copy.27
  317.1 0.0 copy-start.1
  317.1 1.4 copy.26
  318.5 0.6 copy-done.1
  319.1 0.0 copy-start
  319.1 1.3 copy.30
  320.4 1.6 copy-done
  322.1 2.0 copy.31
Async XLA Ops:
  317.1 2.0 copy-start.1
  319.1 2.9 copy-start

commit v2 on v1

--- a/solution.py
+++ b/solution.py
@@ -213,7 +213,7 @@
     )
 
 
-VMEM_BYTES = 62 * 2**20
+VMEM_BYTES = 64 * 2**20
 MESH = pl.DeviceIdType.MESH
 f32 = jnp.float32
 bf16 = jnp.bfloat16
@@ -224,6 +224,23 @@
 N1, N2, DF, DO = range(4)
 
 
+def rem(a, b):
+    return a % b if isinstance(a, int) else lax.rem(a, b)
+
+
+def div(a, b):
+    return a // b if isinstance(a, int) else lax.div(a, b)
+
+
+def cases(value, branches):
+    for low, high, fn in branches:
+        if isinstance(value, int):
+            if low <= value < high:
+                fn()
+        else:
+            pl.when((value >= low) & (value < high))(fn)
+
+
 def mm(lhs, rhs, dims=NN):
     return lax.dot_general(lhs, rhs, dims, preferred_element_type=f32)
 
@@ -231,18 +248,21 @@
 def fused(
     dims,
     stream_in, norm_gain, win, taps, wout, ffn_gain, wgate, wup, wdown, out_grad,
-    out_stream, out_sgrad, out_units, out_small,
-    L, R, WIN, WOUT, WG, WU, WD, H, RATE, PB, PR, XR,
-    GA, GB, RA0, RA1, RA2, RB0, RB1, RB2, RT, FO,
-    EXT, DYE, CF, HALO, DHALO, GAIN, TAPS, GACC, CACC, SMR,
-    load_sem, ps, pr, xs, xr, ags, agr, hs, hr, rss, rsr, fos, oss, sms, smr,
+    out_stream, out_sgrad, out_norm, out_in, out_conv, out_out, out_ffn, out_gate, out_up, out_down,
+    L, R, WIN, WOUT, WG, WU, WD, H, DH, RATE, PB, PR, XR,
+    GA, GB, RA0, RA1, RA2, RB0, RB1, RB2, RT, FO, FT, SM,
+    EXT, DYE, HALO, DHALO, GAIN, TAPS, GACC, CACC, SMR,
+    load_sem, ps, pr, xs, xr, ags, agr, hs, dhs, hr, rss, rsr, fos, oss, sts, str_, sms, smr,
 ):
     M, TOK, D, C, F, U = dims
     half = TOK // 2
     CS, CA, CB, CP, CZ = 0, F, 2 * F, 3 * F, 3 * F + 3 * C
     UNITS = 2 * (-(-(CZ + C) // U))
     PER = UNITS // 2
-    rows_of = (GA.shape[2], GB.shape[2])
+    full = (U, GA.shape[2], GB.shape[2])
+    width = CZ + C - (PER - 1) * U
+    tail_b = width // 6 // 16 * 16 + 16 * (width % 96 > 0)
+    short = (width, width - tail_b, tail_b)
     seq = lax.axis_index("seq")
     tp = lax.axis_index("tp")
     n = lax.axis_size("seq")
@@ -343,7 +363,7 @@
             hid = H[m, loc] + total
             H[m, loc] = hid
             rate = rate_of(hid)
-            RATE[l, which, m, loc] = rate
+            RATE[m, loc, 2 * l + which : 2 * l + which + 1] = rate
             L[l, kind, m, rows] = (hid * rate * gain).astype(bf16)
 
         rows_loop(m, body)
@@ -353,7 +373,7 @@
         ref = PB.at[m, mine]
         return (
             pltpu.make_async_copy(ref, out_stream.at[m, mine], oss.at[m]),
-            remote(ref, out_stream.at[m, mine], ags.at[m], agr.at[m], sib),
+            remote(ref, out_stream.at[m, mine], sts.at[m], str_.at[m], sib),
         )
 
     def finish_stream(m):
@@ -376,15 +396,15 @@
             prod = total * nrm
             GACC[2 * which + l] += prod[0:8] + prod[8:16] + prod[16:24] + prod[24:32]
             mean = jnp.mean(prod * gain, axis=-1, keepdims=True)
-            emit(loc, rows, RATE[l, which, m, loc] * (total * gain - nrm * mean))
+            emit(loc, rows, RATE[m, loc, 2 * l + which : 2 * l + which + 1] * (total * gain - nrm * mean))
 
         rows_loop(m, body)
 
     def finish_dn2(l, m):
         def emit(loc, rows, delta):
-            prev = L[1, DF, m, rows].astype(f32) if l == 1 else H[m, loc]
+            prev = L[1, DF, m, rows].astype(f32) if l == 1 else DH[m, loc]
             new = prev + delta
-            H[m, loc] = new
+            DH[m, loc] = new
             L[l, DO, m, rows] = new.astype(bf16)
 
         norm_back(l, 1, N2, m, emit)
@@ -392,8 +412,8 @@
 
     def finish_dn1(l, m):
         def emit(loc, rows, delta):
-            new = H[m, loc] + delta
-            H[m, loc] = new
+            new = DH[m, loc] + delta
+            DH[m, loc] = new
             if l == 1:
                 L[0, DF, m, rows] = new.astype(bf16)
 
@@ -406,8 +426,8 @@
 
     def grad_copies(m):
         return (
-            pltpu.make_async_copy(H.at[m], out_sgrad.at[m, mine], oss.at[m]),
-            remote(H.at[m], out_sgrad.at[m, mine], ags.at[m], agr.at[m], sib),
+            pltpu.make_async_copy(DH.at[m], out_sgrad.at[m, mine], oss.at[m]),
+            remote(DH.at[m], out_sgrad.at[m, mine], ags.at[m], agr.at[m], sib),
         )
 
     def put_partial(m, tile):
@@ -423,7 +443,7 @@
         return remote(EXT.at[pl.ds(TOK, 8)], HALO.at[l, m], hs, hr.at[0, l, m], nxt)
 
     def dhcopy(l, m):
-        return remote(DYE.at[pl.ds(0, 8)], DHALO.at[l, m], hs, hr.at[1, l, m], prv)
+        return remote(DYE.at[rem(m, 2), pl.ds(0, 8)], DHALO.at[l, m], dhs.at[rem(m, 2)], hr.at[1, l, m], prv)
 
     def tap(l, k):
         return TAPS[k, l : l + 1, :]
@@ -440,7 +460,7 @@
             gain = GAIN[0, 0:1, :]
             hid = L[0, N1, m, mine].astype(f32)
             H[m] = hid
-            RATE[0, 0, m] = rate_of(hid)
+            RATE[m, :, 0:1] = rate_of(hid)
 
             def chunk(i, _):
                 rows = pl.ds(pl.multiple_of(i * 32, 32), 32)
@@ -460,27 +480,25 @@
         hcopy(l, m).start()
         cgate = mm(first, WIN[l, :, C : 2 * C])
         R[l, m, :, CP + C : CP + 2 * C] = cgate.astype(bf16)
-        CF[...] = cgate
+        DYE[0, 0:TOK] = cgate
 
     def conv_fwd_b(l, m):
         hcopy(l, m).wait()
-        R[l, m, :, CZ : CZ + C] = (CF[...] * conv_now(l, m)).astype(bf16)
+        R[l, m, :, CZ : CZ + C] = (DYE[0, 0:TOK] * conv_now(l, m)).astype(bf16)
         gated = R[l, m, :, CZ : CZ + C]
         put_partial(m, lambda cols: mm(gated, WOUT[l, :, cols]))
 
-    def ffn_tiles(body):
+    def ffn_tiles(body, low=0, high=None):
         def step(t, _):
             body(pl.multiple_of(t * U, 128))
             return 0
 
-        lax.fori_loop(0, F // U, step, 0)
-
-    def ffn_fwd(l, m):
-        agcopy(l, N2, m).wait()
-        second = L[l, N2, m]
-
+        lax.fori_loop(low, F // U if high is None else high, step, 0)
+
+    def ffn_fwd(l, m, low=0, high=None):
         def body(off):
             cols = pl.ds(off, U)
+            second = L[l, N2, m]
             a = mm(second, WG[:, cols])
             b = mm(second, WU[:, cols])
             sig = jax.nn.sigmoid(a)
@@ -494,14 +512,14 @@
                 R[l, m, :, pl.ds(CA + off, U)] = (ds * b * sig * (1.0 + a * (1.0 - sig))).astype(bf16)
                 R[l, m, :, pl.ds(CB + off, U)] = (ds * silu).astype(bf16)
 
-        ffn_tiles(body)
+        ffn_tiles(body, low, high)
+
+    def ffn_down(l, m):
         act = R[l, m, :, CS : CS + F]
         put_partial(m, lambda cols: mm(act, WD[:, cols]))
 
     def ffn_bwd(l, m):
         if l == 0:
-            agcopy(0, DF, m).wait()
-
             def body(off):
                 a = R[l, m, :, pl.ds(CA + off, U)].astype(f32)
                 b = R[l, m, :, pl.ds(CB + off, U)].astype(f32)
@@ -511,21 +529,17 @@
                 R[l, m, :, pl.ds(CB + off, U)] = (ds * a * sig).astype(bf16)
 
             ffn_tiles(body)
-        else:
-            for cp in stream_copies(m):
-                cp.wait()
         da = R[l, m, :, CA : CA + F]
         db = R[l, m, :, CB : CB + F]
         put_partial(m, lambda cols: mm(da, WG[cols, :], NT) + mm(db, WU[cols, :], NT))
 
     def conv_bwd_a(l, m):
-        agcopy(l, DO, m).wait()
         dz = mm(L[l, DO, m], WOUT[l], NT)
         bgate = R[l, m, :, CP : CP + C].astype(f32)
         xin = R[l, m, :, CP + 2 * C : CP + 3 * C].astype(f32)
         EXT[8 : 8 + TOK] = (bgate * xin).astype(bf16).astype(f32)
         dy = dz * R[l, m, :, CP + C : CP + 2 * C].astype(f32)
-        DYE[0:TOK] = dy
+        DYE[rem(m, 2), 0:TOK] = dy
         dhcopy(l, m).start()
         R[l, m, :, CP + C : CP + 2 * C] = (dz * conv_now(l, m)).astype(bf16)
         for k in range(3):
@@ -534,8 +548,11 @@
 
     def conv_bwd_b(l, m):
         dhcopy(l, m).wait()
-        DYE[TOK : TOK + 8] = jnp.where(seq == n - 1, 0.0, DHALO[l, m])
-        dbx = tap(l, 2) * DYE[0:TOK] + tap(l, 1) * DYE[1 : 1 + TOK] + tap(l, 0) * DYE[2 : 2 + TOK]
+        s = rem(m, 2)
+        DYE[s, TOK : TOK + 8] = jnp.where(seq == n - 1, 0.0, DHALO[l, m])
+        dbx = (
+            tap(l, 2) * DYE[s, 0:TOK] + tap(l, 1) * DYE[s, 1 : 1 + TOK] + tap(l, 0) * DYE[s, 2 : 2 + TOK]
+        )
         bgate = R[l, m, :, CP : CP + C].astype(f32)
         xin = R[l, m, :, CP + 2 * C : CP + 3 * C].astype(f32)
         R[l, m, :, CP : CP + C] = (dbx * xin).astype(bf16)
@@ -549,133 +566,168 @@
         b = [bits[o] for o in ORDERS[lane]]
         return [b[0] * 4, b[0] * 4 + b[1] * 2, b[0] * 4 + b[1] * 2 + b[2]][step]
 
-    def rs_copy(lane, step, t):
+    def sized(t, fn):
+        cases(rem(t, PER), [(0, PER - 1, lambda: fn(full)), (PER - 1, PER, lambda: fn(short))])
+
+    def rs_copy(lane, step, t, rows):
         G, recv = lanes[lane]
-        slot = lax.rem(t, SLOTS)
+        slot = rem(t, SLOTS)
         size = 4 >> step
         o = ORDERS[lane][step]
         off = keep(lane, step) + size - 2 * size * bits[o]
+        cut = pl.ds(0, rows[1 + lane])
         return remote(
-            G.at[slot, pl.ds(off, size)], recv[step].at[slot],
+            G.at[slot, pl.ds(off, size), cut], recv[step].at[slot, :, cut],
             rss.at[lane, step, slot], rsr.at[lane, step, slot], parts[o],
         )
 
     def rs_gen(t):
-        l = 1 - lax.div(t, PER)
-        v = lax.rem(t, PER)
+        l = 1 - div(t, PER)
+        v = rem(t, PER)
         fu = F // U
         kind = jnp.where(v < fu, DF, jnp.where(v < 3 * fu, N2, jnp.where(v < PER - 1, N1, DO)))
-        slot = lax.rem(t, SLOTS)
-        cols = pl.ds(pl.multiple_of(v * U, 128), U)
-        for m in range(M):
-            RT[:, m * TOK : (m + 1) * TOK] = R[l, m, :, cols].T
-
-        def step(j, _):
-            src = L[l, kind, :, :, pl.ds(pl.multiple_of(j * 256, 256), 256)].reshape(M * TOK, 256)
-            res = mm(RT[...], src).astype(bf16)
-            hi, lo = lax.div(j, 2), lax.rem(j, 2)
-            cut = rows_of[0]
-            for y in range(2):
-                block = res[:, y * 128 : (y + 1) * 128]
-                GA[slot, y * 4 + lo * 2 + hi] = block[:cut]
-                GB[slot, lo * 4 + hi * 2 + y] = block[cut:]
-            return 0
-
-        lax.fori_loop(0, D // 256, step, 0)
-        for lane in range(2):
-            rs_copy(lane, 0, t).start()
+        slot = rem(t, SLOTS)
+
+        def make(rows):
+            wide, cut, _ = rows
+            start = v * U if isinstance(v, int) else pl.multiple_of(v * U, 128)
+            for m in range(M):
+                RT[0:wide, m * TOK : (m + 1) * TOK] = R[l, m, :, pl.ds(start, wide)].T
+
+            def step(j, _):
+                src = L[l, kind, :, :, pl.ds(pl.multiple_of(j * 256, 256), 256)].reshape(M * TOK, 256)
+                res = mm(RT[0:wide], src).astype(bf16)
+                hi, lo = lax.div(j, 2), lax.rem(j, 2)
+                for y in range(2):
+                    block = res[:, y * 128 : (y + 1) * 128]
+                    GA[slot, y * 4 + lo * 2 + hi, 0:cut] = block[:cut]
+                    GB[slot, lo * 4 + hi * 2 + y, 0 : wide - cut] = block[cut:]
+                return 0
+
+            lax.fori_loop(0, D // 256, step, 0)
+            for lane in range(2):
+                rs_copy(lane, 0, t, rows).start()
+
+        sized(t, make)
 
     def rs_add(step, t):
-        slot = lax.rem(t, SLOTS)
-        for lane in range(2):
-            G, recv = lanes[lane]
-            rs_copy(lane, step, t).wait()
-            base = keep(lane, step)
-
-            def add(i, _):
-                G[slot, base + i] = (
-                    G[slot, base + i].astype(f32) + recv[step][slot, i].astype(f32)
-                ).astype(bf16)
-                return 0
-
-            lax.fori_loop(0, 4 >> step, add, 0)
-            rs_copy(lane, step + 1, t).start()
-
-    def unit_copy(t):
-        l = 1 - lax.div(t, PER)
-        v = lax.rem(t, PER)
-        s = lax.rem(t, 2)
-        return pltpu.make_async_copy(
-            FO.at[s], out_units.at[l, pl.ds(pl.multiple_of(v * U, 128), U)], fos.at[s]
-        )
+        slot = rem(t, SLOTS)
+
+        def go(rows):
+            for lane in range(2):
+                G, recv = lanes[lane]
+                rs_copy(lane, step, t, rows).wait()
+                base = keep(lane, step)
+                cut = rows[1 + lane]
+
+                def add(i, _):
+                    G[slot, base + i, 0:cut] = (
+                        G[slot, base + i, 0:cut].astype(f32) + recv[step][slot, i, 0:cut].astype(f32)
+                    ).astype(bf16)
+                    return 0
+
+                lax.fori_loop(0, 4 >> step, add, 0)
+                rs_copy(lane, step + 1, t, rows).start()
+
+        sized(t, go)
+
+    def unit_copies(t, which):
+        l = 1 - div(t, PER)
+        v = rem(t, PER)
+        fu = F // U
+
+        def at(first):
+            return pl.ds((v - first) * U if isinstance(v, int) else pl.multiple_of((v - first) * U, 128), U)
+
+        if which == 0:
+            pairs = [(FO, out_down.at[l, at(0)])]
+        elif which == 1:
+            pairs = [(FT, out_gate.at[l, :, at(fu)])]
+        elif which == 2:
+            pairs = [(FT, out_up.at[l, :, at(2 * fu)])]
+        elif which == 3:
+            pairs = [(FT.at[:, pl.ds(0, C)], out_in.at[l, 0]),
+                     (FT.at[:, pl.ds(C, U - C)], out_in.at[l, 1, :, pl.ds(0, U - C)])]
+        elif which == 4:
+            pairs = [(FT.at[:, pl.ds(0, 2 * C - U)], out_in.at[l, 1, :, pl.ds(U - C, 2 * C - U)]),
+                     (FT.at[:, pl.ds(2 * C - U, C)], out_in.at[l, 2])]
+        else:
+            pairs = [(FO.at[pl.ds(0, width)], out_out.at[l])]
+        return [pltpu.make_async_copy(a, b, fos.at[i]) for i, (a, b) in enumerate(pairs)]
+
+    def by_target(t, fn):
+        fu = F // U
+        edges = (0, fu, 2 * fu, 3 * fu, 3 * fu + 1, 3 * fu + 2, PER)
+        cases(rem(t, PER), [(edges[i], edges[i + 1], functools.partial(fn, i)) for i in range(6)])
+
+    def unit_wait(t):
+        def go(which):
+            for cp in unit_copies(t, which):
+                cp.wait()
+
+        by_target(t, go)
 
     def rs_last(t):
-        slot = lax.rem(t, SLOTS)
-        s = lax.rem(t, 2)
-        for lane in range(2):
-            rs_copy(lane, 2, t).wait()
-
-        @pl.when(t >= 2)
-        def _():
-            unit_copy(t - 2).wait()
-
-        cut = rows_of[0]
-        FO[s, 0:cut] = GA[slot, keep(0, 2)].astype(f32) + RA2[slot, 0].astype(f32)
-        FO[s, cut:U] = GB[slot, keep(1, 2)].astype(f32) + RB2[slot, 0].astype(f32)
-        unit_copy(t).start()
-
-    def tick(t):
-        static = isinstance(t, int)
-
-        def at(cond, fn, arg):
-            if static:
-                if cond(t):
-                    fn(jnp.int32(arg))
+        slot = rem(t, SLOTS)
+        if isinstance(t, int):
+            if t >= 1:
+                unit_wait(t - 1)
+        else:
+            pl.when(t >= 1)(lambda: unit_wait(t - 1))
+
+        def go(rows):
+            wide, cut, _ = rows
+            for lane in range(2):
+                rs_copy(lane, 2, t, rows).wait()
+            FO[0:cut] = GA[slot, keep(0, 2), 0:cut].astype(f32) + RA2[slot, 0, 0:cut].astype(f32)
+            FO[cut:wide] = (
+                GB[slot, keep(1, 2), 0 : wide - cut].astype(f32) + RB2[slot, 0, 0 : wide - cut].astype(f32)
+            )
+
+        sized(t, go)
+
+        def send(which):
+            if which in (1, 2, 3, 4):
+                FT[...] = FO[...].T
+            for cp in unit_copies(t, which):
+                cp.start()
+
+        by_target(t, send)
+
+    def tick_gen(t):
+        if not isinstance(t, int) or t < UNITS:
+            rs_gen(t)
+
+    def tick_rest(t):
+        steps = (functools.partial(rs_add, 0), functools.partial(rs_add, 1), rs_last)
+        for lag, fn in enumerate(steps, 1):
+            if isinstance(t, int):
+                if 0 <= t - lag < UNITS:
+                    fn(t - lag)
             else:
-                pl.when(cond(t))(lambda: fn(arg))
-
-        at(lambda q: q < UNITS, rs_gen, t)
-        at(lambda q: (q >= 1) & (q < UNITS + 1), functools.partial(rs_add, 0), t - 1)
-        at(lambda q: (q >= 2) & (q < UNITS + 2), functools.partial(rs_add, 1), t - 2)
-        at(lambda q: (q >= 3) & (q < UNITS + 3), rs_last, t - 3)
-
-    finishers = [
-        lambda m: finish_norm(0, 1, N2, m),
-        lambda m: finish_norm(1, 0, N1, m),
-        lambda m: finish_norm(1, 1, N2, m),
-        finish_stream,
-        lambda m: finish_dn2(1, m),
-        lambda m: finish_dn1(1, m),
-        lambda m: finish_dn2(0, m),
-        lambda m: finish_dn1(0, m),
-    ]
-
-    def behind(p, m):
-        @pl.when((m > 0) | (p > 0))
-        def _():
+                pl.when(t >= lag)(functools.partial(fn, t - lag))
+
+    def behind(prev, cur, m):
+        if prev is None:
+            pl.when(m > 0)(lambda: mid(m - 1))
+        else:
             mid(lax.rem(m + M - 1, M))
-
-        if p > 0:
-            @pl.when(m < 2)
-            def _():
-                finishers[p - 1](m + M - 2)
-
-        @pl.when(m >= 2)
-        def _():
-            finishers[p](m - 2)
-
-    def phase(p, first, second, tick_base=None):
+            pl.when(m < 2)(lambda: prev(m + M - 2))
+        pl.when(m >= 2)(lambda: cur(m - 2))
+
+    def phase(prev, cur, first, second=None, tick=None, ahead=None):
         def step(m, _):
-            first(m)
-            if second is None:
-                behind(p, m)
-                if tick_base is not None:
-                    tick(tick_base + m)
-            else:
-                if tick_base is not None:
-                    tick(tick_base + m)
-                behind(p, m)
+            if ahead is not None:
+                ahead(m)
+            if tick is not None:
+                tick_gen(tick + m)
+            if first is not None:
+                first(m)
+            behind(prev, cur, m)
+            if second is not None:
                 second(m)
+            if tick is not None:
+                tick_rest(tick + m)
             return 0
 
         lax.fori_loop(0, M, step, 0)
@@ -684,55 +736,140 @@
         for cp in copies:
             cp.wait()
 
+    end_o0 = functools.partial(finish_norm, 0, 1, N2)
+    end_f0 = functools.partial(finish_norm, 1, 0, N1)
+    end_o1 = functools.partial(finish_norm, 1, 1, N2)
+    end_n1 = functools.partial(finish_dn2, 1)
+    end_c1 = functools.partial(finish_dn1, 1)
+    end_n0 = functools.partial(finish_dn2, 0)
+    end_c0 = functools.partial(finish_dn1, 0)
+
     arrived(load_conv(0))
-    phase(0, lambda m: conv_fwd_a(0, m), lambda m: conv_fwd_b(0, m))
+    phase(None, end_o0, lambda m: conv_fwd_a(0, m), lambda m: conv_fwd_b(0, m))
     arrived(load_ffn(0))
-    phase(1, lambda m: ffn_fwd(0, m), None)
+
+    def f0(m):
+        agcopy(0, N2, m).wait()
+        ffn_fwd(0, m)
+        ffn_down(0, m)
+
+    phase(end_o0, end_f0, f0)
     for cp in load_ffn(1):
         cp.start()
     arrived(load_conv(1))
-    phase(2, lambda m: conv_fwd_a(1, m), lambda m: conv_fwd_b(1, m))
+    phase(end_f0, end_o1, lambda m: conv_fwd_a(1, m), lambda m: conv_fwd_b(1, m))
     arrived(load_ffn(1) + [load_og])
-    phase(3, lambda m: ffn_fwd(1, m), None)
-    phase(4, lambda m: ffn_bwd(1, m), None, 0)
+
+    agcopy(1, N2, 0).wait()
+    ffn_fwd(1, 0)
+    mid(M - 1)
+    end_o1(M - 2)
+    agcopy(1, N2, 1).wait()
+    ffn_fwd(1, 1)
+    agcopy(1, N2, 2).wait()
+    ffn_fwd(1, 2, 0, 2)
+    end_o1(M - 1)
+    ffn_fwd(1, 2, 2)
+    agcopy(1, N2, 3).wait()
+    ffn_fwd(1, 3)
+    tick_gen(0)
+
+    def start_c1(m):
+        agcopy(1, DO, m).wait()
+        conv_bwd_a(1, m)
+
+    def last_only(fn):
+        return lambda m: pl.when(m == M - 1)(lambda: fn(0))
+
+    def next_one(fn):
+        return lambda m: pl.when(m < M - 1)(lambda: fn(m + 1))
+
+    phase(None, end_n1, lambda m: ffn_bwd(1, m), tick=1, ahead=last_only(start_c1))
     for cp in load_ffn(0):
         cp.start()
-    phase(5, lambda m: conv_bwd_a(1, m), lambda m: conv_bwd_b(1, m), M)
+    phase(end_n1, end_c1, None, lambda m: conv_bwd_b(1, m), tick=1 + M, ahead=next_one(start_c1))
     arrived(load_ffn(0))
-    phase(6, lambda m: ffn_bwd(0, m), None, 2 * M)
-    phase(7, lambda m: conv_bwd_a(0, m), lambda m: conv_bwd_b(0, m), 3 * M)
+
+    def n0(m):
+        ffn_bwd(0, m)
+
+    def n0_tick(m, _):
+        pl.when(m == 0)(lambda: agcopy(0, DF, 0).wait())
+        pl.when(m == 1)(lambda: agcopy(0, DF, 1).wait())
+
+        @pl.when(m == 2)
+        def _():
+            agcopy(0, DF, 2).wait()
+            agcopy(0, DF, 3).wait()
+
+        tick_gen(1 + 2 * M + m)
+        n0(m)
+        behind(end_c1, end_n0, m)
+        tick_rest(1 + 2 * M + m)
+        return 0
+
+    lax.fori_loop(0, M, n0_tick, 0)
+    load_ffn(1)[2].start()
+    load_ffn(1)[2].wait()
+
+    def f1(m):
+        agcopy(0, DO, m).wait()
+        ffn_down(1, m)
+
+    def start_c0(m):
+        conv_bwd_a(0, m)
+
+    phase(end_n0, finish_stream, f1, tick=1 + 3 * M, ahead=last_only(start_c0))
+
+    def c0(m):
+        for cp in stream_copies(m):
+            cp.wait()
+        conv_bwd_b(0, m)
+
+    phase(finish_stream, end_c0, None, c0, tick=1 + 4 * M, ahead=next_one(start_c0))
+    t = 1 + 5 * M
+    tick_gen(t)
     mid(M - 1)
-    finishers[7](M - 2)
-    tick(4 * M)
-    finishers[7](M - 1)
+    end_c0(M - 2)
+    tick_rest(t)
+    tick_gen(t + 1)
+    end_c0(M - 1)
 
     for i in range(4):
-        out_small[i : i + 1] = jnp.sum(GACC[i], axis=0, keepdims=True)
-    out_small[4:8] = jnp.zeros((4, D), f32)
+        SM[i : i + 1] = jnp.sum(GACC[i], axis=0, keepdims=True)
+    SM[4:8] = jnp.zeros((4, D), f32)
     for l in range(2):
         for k in range(3):
-            out_small[4 + l : 5 + l, k * C : (k + 1) * C] = jnp.sum(CACC[l, k], axis=0, keepdims=True)
+            SM[4 + l : 5 + l, k * C : (k + 1) * C] = jnp.sum(CACC[l, k], axis=0, keepdims=True)
 
     def small(i):
-        return remote(out_small, SMR.at[i], sms.at[i], smr.at[i], [sib, *parts][i])
+        return remote(SM, SMR.at[i], sms.at[i], smr.at[i], [sib, *parts][i])
 
     small(0).start()
-    t = 4 * M + 1
+    tick_rest(t + 1)
+    t += 2
     for i in range(4):
-        tick(t)
-        t += 1
+        tick_gen(t)
         small(i).wait()
         if i == 0:
-            out_small[0:4] += SMR[0, 0:4]
+            SM[0:4] += SMR[0, 0:4]
         else:
-            out_small[...] += SMR[i]
+            SM[...] += SMR[i]
         if i < 3:
             small(i + 1).start()
+        tick_rest(t)
+        t += 1
     while t < UNITS + 3:
-        tick(t)
+        tick_gen(t)
+        tick_rest(t)
         t += 1
-    for q in (UNITS - 2, UNITS - 1):
-        unit_copy(jnp.int32(q)).wait()
+    own = pl.ds(pl.multiple_of(tp * C, 128), C)
+    out_norm[...] = SM[0:2, own]
+    out_ffn[...] = SM[2:4, own]
+    for l in range(2):
+        for k in range(3):
+            out_conv[k, l : l + 1, :] = SM[4 + l : 5 + l, k * C : (k + 1) * C]
+    unit_wait(UNITS - 1)
     for m in range(M):
         for cp in grad_copies(m):
             cp.wait()
@@ -742,7 +879,6 @@
     M, TOK, D = stream_in.shape
     C, F = wout.shape[1], wgate.shape[2]
     U = 384
-    per = -(-(3 * F + 4 * C) // U)
     rb = U // 6
     ra = U - rb
     half = TOK // 2
@@ -756,21 +892,28 @@
         out_shape=[
             jax.ShapeDtypeStruct((M, TOK, D), bf16),
             jax.ShapeDtypeStruct((M, TOK, D), f32),
-            jax.ShapeDtypeStruct((LAYERS, per * U, 128), f32),
-            jax.ShapeDtypeStruct((8, D), f32),
+            jax.ShapeDtypeStruct((LAYERS, C), f32),
+            jax.ShapeDtypeStruct((LAYERS, 3, 128, C), f32),
+            jax.ShapeDtypeStruct((3, LAYERS, C), f32),
+            jax.ShapeDtypeStruct((LAYERS, C, 128), f32),
+            jax.ShapeDtypeStruct((LAYERS, C), f32),
+            jax.ShapeDtypeStruct((LAYERS, 128, F), f32),
+            jax.ShapeDtypeStruct((LAYERS, 128, F), f32),
+            jax.ShapeDtypeStruct((LAYERS, F, 128), f32),
         ],
         in_specs=[anys, vmem, anys, vmem, anys, vmem, anys, anys, anys, anys],
-        out_specs=[anys, anys, anys, vmem],
+        out_specs=[anys, anys, vmem, anys, vmem, anys, vmem, anys, anys, anys],
         scratch_shapes=[
             vm((LAYERS, 4, M, TOK, D), bf16),
-            vm((LAYERS, M, TOK, per * U), bf16),
+            vm((LAYERS, M, TOK, 3 * F + 4 * C), bf16),
             vm((LAYERS, D, 3 * C), bf16),
             vm((LAYERS, C, D), bf16),
             vm((D, F), bf16),
             vm((D, F), bf16),
             vm((F, D), bf16),
             vm((M, half, D), f32),
-            vm((LAYERS, 2, M, half, 1), f32),
+            vm((M, half, D), f32),
+            vm((M, half, 2 * LAYERS), f32),
             vm((M, TOK, D), bf16),
             vm((M, half, D), bf16),
             vm((M, half, D), bf16),
@@ -783,10 +926,11 @@
             vm((S, 2, rb, 128), bf16),
             vm((S, 1, rb, 128), bf16),
             vm((U, M * TOK), bf16),
-            vm((2, U, 128), f32),
+            vm((U, 128), f32),
+            vm((128, U), f32),
+            vm((8, D), f32),
             vm((TOK + 8, C), f32),
-            vm((TOK + 8, C), f32),
-            vm((TOK, C), f32),
+            vm((2, TOK + 8, C), f32),
             vm((LAYERS, M, 8, C), f32),
             vm((LAYERS, M, 8, C), f32),
             vm((4, LAYERS, D), f32),
@@ -796,9 +940,9 @@
             vm((4, 8, D), f32),
             dma((16,)),
             dma((M,)), dma((M,)), dma((M,)), dma((M,)), dma((M,)), dma((M,)),
-            dma, dma((2, LAYERS, M)),
+            dma, dma((2,)), dma((2, LAYERS, M)),
             dma((2, 3, S)), dma((2, 3, S)),
-            dma((2,)), dma((M,)), dma((4,)), dma((4,)),
+            dma((2,)), dma((M,)), dma((M,)), dma((M,)), dma((4,)), dma((4,)),
         ],
         name="fused",
         compiler_params=pltpu.CompilerParams(
@@ -810,21 +954,12 @@
 def body_fused(
     stream_in, norm_gain, in_proj, conv_taps, out_proj, ffn_gain, gate_proj, up_proj, down_proj, out_grad
 ):
-    C, F = out_proj.shape[1], gate_proj.shape[2]
-    D = stream_in.shape[2]
-    out_stream, out_sgrad, units, small = fused_call(
+    (out_stream, out_sgrad, norm_g, in_g, conv_g, out_g, ffn_g, gate_g, up_g, down_g) = fused_call(
         stream_in, norm_gain, jnp.transpose(in_proj, (0, 2, 1, 3)), jnp.transpose(conv_taps, (1, 0, 2)),
         out_proj, ffn_gain, gate_proj, up_proj, down_proj, out_grad,
     )
-    offset = lax.axis_index("tp") * C
-    norm_g = lax.dynamic_slice_in_dim(small[0:2], offset, C, axis=1)
-    ffn_g = lax.dynamic_slice_in_dim(small[2:4], offset, C, axis=1)
-    conv_g = small[4:6, : 3 * C].reshape(LAYERS, 3, C)
-    down_g = units[:, :F]
-    gate_g = jnp.swapaxes(units[:, F : 2 * F], 1, 2)
-    up_g = jnp.swapaxes(units[:, 2 * F : 3 * F], 1, 2)
-    in_g = units[:, 3 * F : 3 * F + 3 * C].reshape(LAYERS, 3, C, 128).transpose(0, 3, 1, 2)
-    out_g = units[:, 3 * F + 3 * C : 3 * F + 4 * C]
+    in_g = jnp.transpose(in_g, (0, 2, 1, 3))
+    conv_g = jnp.transpose(conv_g, (1, 0, 2))
     return (out_stream, out_sgrad, norm_g, in_g, conv_g, out_g, ffn_g, gate_g, up_g, down_g)
 
 

time: 325 us -> 297 us (0.914)
  Pallas kernels: 305 us -> 285 us
  local copies, waits for them, and re-layouts: 18.3 us -> 11.7 us
    pallas_call x1, Pallas kernels: 305 us -> 285 us  [fused_call(): pl.pallas_call(functools.partial(fused, (M, TOK, D, C, F, U)), out_shape=...]
    slice x5 -> x0, local copies, waits for them, and re-layouts: 8.26 us -> none  [the longest x1 3.23 us: body_fused(): down_g = units[:, :F]]
    unnamed x8 -> x28, local copies, waits for them, and re-layouts: 8.35 us -> 11.7 us
where the time goes in v2:
time: 297 us
  Pallas kernels  285 us (96%)
  local copies, waits for them, and re-layouts  11.7 us (4%)
    pallas_call x1, Pallas kernels, fused_call(): pl.pallas_call(functools.partial(fused, (M, TOK, D, C, F, U)), out_shape=...  285 us
    unnamed x28, local copies, waits for them, and re-layouts  11.7 us

profile of v2, /device:TPU:0, one launch (start us, length us, event | category | flops | bytes accessed | tf_op | source)
XLA Modules:
  0.0 297.0 jit_solution(1537414127824117308)
XLA Ops:
  0.6 284.7 %fused.1 = (bf16[4,256,1024]{2,1,0:T(8,128)(2,1)}, f32[4,256,1024]{2,1,0:T(8,128)}, f32[2,256]{1,0:T(2,128)}, f32[2,3,128,256]{3,2,1,0:T(8,128)}, f32[3,2,256]{2...) custom-call(bf16[4,256,1024]{2,1,0:T(8,128)(2,1)} %stream_in.1, ...), custom_call_target="tpu_custom_call" | custom-call | tf_op jit(solution)/shard_map/fused/pallas_call | solution.py:890
  285.3 0.0 copy-start
  285.3 3.2 %copy.30 = bf16[4,256,1024]{2,1,0:T(8,128)(2,1)} copy(bf16[4,256,1024]{2,1,0:T(8,128)(2,1)} %get-tuple-element.40) | data formatting | bytes 4194304
  288.6 0.0 copy-done
  288.6 0.0 copy-start.8
  288.6 0.0 copy-start.4
  288.6 0.0 copy-start.5
  288.6 2.0 copy.31
  290.6 0.0 copy-done.8
  290.6 0.6 copy.32
  291.2 0.0 copy-done.4
  291.2 0.9 copy.33
  292.1 0.0 copy-done.6
  292.1 0.6 copy.34
  292.7 0.0 copy-done.5
  292.7 0.7 copy.35
  293.4 0.0 copy-done.7
  293.4 0.6 copy.36
  293.9 0.0 copy-done.3
  294.0 1.0 copy.37
  295.0 0.0 copy-done.2
  295.0 1.0 copy.38
  296.0 0.0 copy-done.1
  296.0 1.0 copy.39
  (5 shorter events, 0.0 us)
Async XLA Ops:
  285.3 3.2 %copy-start = (f32[4,256,1024]{2,1,0:T(8,128)S(1)}, f32[4,256,1024]{2,1,0:T(8,128)}, u32[]{:S(2)}) copy-start(f32[4,256,1024]{2,1,0:T(8,128)} %get-tuple-element.41) | copy-start | bytes 12582916
  288.6 2.0 copy-start.8
  288.6 2.6 copy-start.4
  288.6 3.5 %copy-start.6 = (f32[3,2,256]{2,1,0:T(2,128)S(1)}, f32[3,2,256]{2,1,0:T(2,128)}, u32[]{:S(2)}) copy-start(f32[3,2,256]{2,1,0:T(2,128)} %get-tuple-element.24) | copy-start | bytes 18436
  288.6 4.1 %copy-start.5 = (f32[2,256,128]{2,1,0:T(8,128)S(1)}, f32[2,256,128]{2,1,0:T(8,128)}, u32[]{:S(2)}) copy-start(f32[2,256,128]{2,1,0:T(8,128)} %get-tuple-element.45) | copy-start | bytes 786436
  290.6 2.8 copy-start.7
  290.6 3.4 %copy-start.3 = (f32[2,128,1152]{2,1,0:T(8,128)S(1)}, f32[2,128,1152]{2,1,0:T(8,128)}, u32[]{:S(2)}) copy-start(f32[2,128,1152]{2,1,0:T(8,128)} %get-tuple-element.47) | copy-start | bytes 3538948
  291.2 3.8 %copy-start.2 = (f32[2,128,1152]{2,1,0:T(8,128)S(1)}, f32[2,128,1152]{2,1,0:T(8,128)}, u32[]{:S(2)}) copy-start(f32[2,128,1152]{2,1,0:T(8,128)} %get-tuple-element.48) | copy-start | bytes 3538948
  294.0 2.0 copy-start.1

commit v3 on v2

--- a/solution.py
+++ b/solution.py
@@ -221,6 +221,7 @@
 NT = (((1,), (1,)), ((), ()))
 ORDERS = ((0, 1, 2), (1, 2, 0))
 SLOTS = 4
+WIDE = 512
 N1, N2, DF, DO = range(4)
 
 
@@ -249,14 +250,14 @@
     dims,
     stream_in, norm_gain, win, taps, wout, ffn_gain, wgate, wup, wdown, out_grad,
     out_stream, out_sgrad, out_norm, out_in, out_conv, out_out, out_ffn, out_gate, out_up, out_down,
-    L, R, WIN, WOUT, WG, WU, WD, H, DH, RATE, PB, PR, XR,
+    L, R, WIN, WOUT, WGU, WD, H, DH, RATE, PB, PR, XR,
     GA, GB, RA0, RA1, RA2, RB0, RB1, RB2, RT, FO, FT, SM,
-    EXT, DYE, HALO, DHALO, GAIN, TAPS, GACC, CACC, SMR,
-    load_sem, ps, pr, xs, xr, ags, agr, hs, dhs, hr, rss, rsr, fos, oss, sts, str_, sms, smr,
+    EXT, DYE, CF, HALO, HALO2, DHALO, GAIN, TAPS, TAPS2, GACC, CACC, SMR,
+    load_sem, ps, pr, xs, xr, ags, agr, hs, dhs, hr, hs2, hr2, gs, gr, rss, rsr, fos, oss, sts, str_, sms, smr,
 ):
     M, TOK, D, C, F, U = dims
     half = TOK // 2
-    CS, CA, CB, CP, CZ = 0, F, 2 * F, 3 * F, 3 * F + 3 * C
+    CS, CA, CP, CZ = 0, F, 3 * F, 3 * F + 3 * C
     UNITS = 2 * (-(-(CZ + C) // U))
     PER = UNITS // 2
     full = (U, GA.shape[2], GB.shape[2])
@@ -286,22 +287,25 @@
         return pltpu.make_async_copy(stream_in.at[m], L.at[0, N1, m], load_sem.at[m])
 
     def load_conv(l):
-        b = 4 + 4 * l
         return [
-            pltpu.make_async_copy(win.at[l, k], WIN.at[l, :, pl.ds(k * C, C)], load_sem.at[b + k])
+            pltpu.make_async_copy(win.at[l, k], WIN.at[:, pl.ds(k * C, C)], load_sem.at[4 + k])
             for k in range(3)
-        ] + [pltpu.make_async_copy(wout.at[l], WOUT.at[l], load_sem.at[b + 3])]
+        ] + [pltpu.make_async_copy(wout.at[l], WOUT, load_sem.at[7])]
 
     def load_ffn(l):
         return [
-            pltpu.make_async_copy(s.at[l], d, load_sem.at[12 + i])
-            for i, (s, d) in enumerate(((wgate, WG), (wup, WU), (wdown, WD)))
+            pltpu.make_async_copy(
+                src.at[l, :, pl.ds(t * U, U)], WGU.at[:, pl.ds((2 * t + i) * U, U)], load_sem.at[10 + 2 * t + i]
+            )
+            for t in range(F // U)
+            for i, src in enumerate((wgate, wup))
         ]
 
-    load_og = pltpu.make_async_copy(out_grad, L.at[1, DF], load_sem.at[15])
-    for m in range(M):
-        load_stream(m).start()
-    for cp in load_conv(0) + load_ffn(0) + load_conv(1) + [load_og]:
+    def load_down(l):
+        return pltpu.make_async_copy(wdown.at[l], WD, load_sem.at[9])
+
+    load_og = pltpu.make_async_copy(out_grad, L.at[1, DF], load_sem.at[8])
+    for cp in load_conv(0) + [load_stream(m) for m in range(M)]:
         cp.start()
 
     barrier = pltpu.get_barrier_semaphore()
@@ -319,6 +323,53 @@
 
     pl.semaphore_wait(barrier, len(others))
 
+    zpos, ypos = lax.div(seq, 2), lax.rem(seq, 2)
+    zfar, znear = lax.rem(zpos + 2, 4), zpos + 1 - 2 * lax.rem(zpos, 2)
+    strip = D // 8
+
+    def piece(s, z):
+        rows = pl.ds(pl.multiple_of(ypos * strip, strip), strip)
+        if s < 3:
+            return L.at[0, DO, 1 + s, rows, pl.ds(pl.multiple_of(z * TOK, TOK), TOK)]
+        return L.at[0, DO, 0, pl.ds(pl.multiple_of(ypos * strip + z * (C // 8), 16), C // 8)]
+
+    def gathers(s, step):
+        def send(i, src, dst, dev):
+            return remote(src, dst, gs.at[s, i], gr.at[s, i], dev)
+
+        if step == 0:
+            if s < 3:
+                src = win.at[1, s, pl.ds(pl.multiple_of(zpos * TOK + ypos * strip, strip), strip)]
+            else:
+                src = wout.at[1, pl.ds(pl.multiple_of(ypos * strip + zpos * (C // 8), 16), C // 8)]
+            return [send(0, src, piece(s, zpos), xpart)]
+        if step == 1:
+            return [send(1, piece(s, zpos), piece(s, zpos), parts[2])]
+        if step == 2:
+            return [send(2 + i, piece(s, z), piece(s, z), parts[1]) for i, z in enumerate((zpos, zfar))]
+        half_ref = L.at[0, DO, (1 + s) % 4, pl.ds(pl.multiple_of(ypos * strip, strip), strip)]
+        return [send(4, half_ref, half_ref, parts[0])]
+
+    def gather_at(j):
+        for s in range(4):
+            for step, when in enumerate((s, s + 2, s + 4, 7 + 2 * s)):
+                if j == when:
+                    for cp in gathers(s, step):
+                        cp.wait()
+                    if step < 3:
+                        for cp in gathers(s, step + 1):
+                            cp.start()
+
+    def gather_dyn(base, m, late):
+        for i in range(M):
+            pl.when(m == i)(functools.partial(gather_at, base + 2 * i + late))
+
+    for s in range(4):
+        for cp in gathers(s, 0):
+            cp.start()
+    tap_copy = remote(TAPS, TAPS2, hs2.at[1], hr2.at[M], xpart)
+    tap_copy.start()
+
     def pcopy(m):
         return remote(PB.at[m, theirs], PR.at[m], ps.at[m], pr.at[m], sib)
 
@@ -342,11 +393,11 @@
         ref = L.at[l, kind, m, mine]
         return remote(ref, ref, ags.at[m], agr.at[m], sib)
 
-    def rows_loop(m, body):
+    def rows_loop(m, body, received=XR):
         def chunk(i, _):
             off = pl.multiple_of(i * 32, 32)
             rows = pl.ds(pl.multiple_of(core * half + off, 32), 32)
-            total = PB[m, rows].astype(f32) + XR[m, pl.ds(off, 32)].astype(f32)
+            total = PB[m, rows].astype(f32) + received[m, pl.ds(off, 32)].astype(f32)
             body(pl.ds(off, 32), rows, total)
             return 0
 
@@ -355,8 +406,11 @@
     def rate_of(val):
         return lax.rsqrt(jnp.mean(val * val, axis=-1, keepdims=True) + EPS)
 
-    def finish_norm(l, which, kind, m):
-        xcopy(m).wait()
+    def finish_norm(l, which, kind, m, within=False):
+        if within:
+            pcopy(m).wait()
+        else:
+            xcopy(m).wait()
         gain = GAIN[which, l : l + 1, :]
 
         def body(loc, rows, total):
@@ -366,7 +420,7 @@
             RATE[m, loc, 2 * l + which : 2 * l + which + 1] = rate
             L[l, kind, m, rows] = (hid * rate * gain).astype(bf16)
 
-        rows_loop(m, body)
+        rows_loop(m, body, PR if within else XR)
         agcopy(l, kind, m).start()
 
     def stream_copies(m):
@@ -432,11 +486,11 @@
 
     def put_partial(m, tile):
         def step(j, _):
-            cols = pl.ds(pl.multiple_of(j * 256, 256), 256)
+            cols = pl.ds(pl.multiple_of(j * WIDE, WIDE), WIDE)
             PB[m, :, cols] = tile(cols).astype(bf16)
             return 0
 
-        lax.fori_loop(0, D // 256, step, 0)
+        lax.fori_loop(0, D // WIDE, step, 0)
         pcopy(m).start()
 
     def hcopy(l, m):
@@ -445,14 +499,23 @@
     def dhcopy(l, m):
         return remote(DYE.at[rem(m, 2), pl.ds(0, 8)], DHALO.at[l, m], dhs.at[rem(m, 2)], hr.at[1, l, m], prv)
 
+    def hcopy2(m):
+        return remote(DYE.at[1, pl.ds(TOK, 8)], HALO2.at[m], hs2.at[0], hr2.at[m], nxt)
+
     def tap(l, k):
         return TAPS[k, l : l + 1, :]
 
+    def conv_of(ext, halo, taps_ref, l):
+        ext[0:8] = jnp.where(seq == 0, 0.0, halo)
+        t = [taps_ref[k, l : l + 1, :] for k in range(3)]
+        return t[0] * ext[6 : 6 + TOK] + t[1] * ext[7 : 7 + TOK] + t[2] * ext[8 : 8 + TOK]
+
     def conv_now(l, m):
-        EXT[0:8] = jnp.where(seq == 0, 0.0, HALO[l, m])
-        return (
-            tap(l, 0) * EXT[6 : 6 + TOK] + tap(l, 1) * EXT[7 : 7 + TOK] + tap(l, 2) * EXT[8 : 8 + TOK]
-        )
+        return conv_of(EXT, HALO[l, m], TAPS, l)
+
+    def other_in(k):
+        blocks = [L[0, DO, 1 + k, :, r * TOK : (r + 1) * TOK] for r in range(D // TOK)]
+        return jnp.concatenate(blocks, axis=0)
 
     def conv_fwd_a(l, m):
         if l == 0:
@@ -472,69 +535,78 @@
         else:
             agcopy(1, N1, m).wait()
         first = L[l, N1, m]
-        bgate = mm(first, WIN[l, :, 0:C])
-        R[l, m, :, CP : CP + C] = bgate.astype(bf16)
-        xin = mm(first, WIN[l, :, 2 * C : 3 * C])
-        R[l, m, :, CP + 2 * C : CP + 3 * C] = xin.astype(bf16)
+        p = mm(first, WIN[...])
+        bgate, cgate, xin = p[:, 0:C], p[:, C : 2 * C], p[:, 2 * C : 3 * C]
+        R[l, m, :, CP : CP + 3 * C] = p.astype(bf16)
         EXT[8 : 8 + TOK] = (bgate * xin).astype(bf16).astype(f32)
         hcopy(l, m).start()
-        cgate = mm(first, WIN[l, :, C : 2 * C])
-        R[l, m, :, CP + C : CP + 2 * C] = cgate.astype(bf16)
         DYE[0, 0:TOK] = cgate
+        if l == 1:
+            p = mm(first, jnp.concatenate([other_in(k) for k in range(3)], axis=1))
+            DYE[1, 8 : 8 + TOK] = (p[:, 0:C] * p[:, 2 * C : 3 * C]).astype(bf16).astype(f32)
+            hcopy2(m).start()
+            CF[...] = p[:, C : 2 * C]
 
     def conv_fwd_b(l, m):
         hcopy(l, m).wait()
-        R[l, m, :, CZ : CZ + C] = (DYE[0, 0:TOK] * conv_now(l, m)).astype(bf16)
-        gated = R[l, m, :, CZ : CZ + C]
-        put_partial(m, lambda cols: mm(gated, WOUT[l, :, cols]))
-
-    def ffn_tiles(body, low=0, high=None):
+        gated = (DYE[0, 0:TOK] * conv_now(l, m)).astype(bf16)
+        R[l, m, :, CZ : CZ + C] = gated
+        if l == 0:
+            put_partial(m, lambda cols: mm(R[l, m, :, CZ : CZ + C], WOUT[:, cols]))
+        else:
+            hcopy2(m).wait()
+            L[0, DF, m, :, 0:C] = (CF[...] * conv_of(DYE.at[1], HALO2[m], TAPS2, l)).astype(bf16)
+            put_partial(
+                m,
+                lambda cols: mm(R[l, m, :, CZ : CZ + C], WOUT[:, cols])
+                + mm(L[0, DF, m, :, 0:C], L[0, DO, 0, :, cols]),
+            )
+
+    def down_back(m):
+        ds = mm(L[1, DF, m], WD[...], NT).astype(bf16)
+        for t in range(F // U):
+            R[1, m, :, CA + (2 * t + 1) * U : CA + (2 * t + 2) * U] = ds[:, t * U : (t + 1) * U]
+
+    def ffn_fwd(l, m):
         def step(t, _):
-            body(pl.multiple_of(t * U, 128))
-            return 0
-
-        lax.fori_loop(low, F // U if high is None else high, step, 0)
-
-    def ffn_fwd(l, m, low=0, high=None):
-        def body(off):
-            cols = pl.ds(off, U)
-            second = L[l, N2, m]
-            a = mm(second, WG[:, cols])
-            b = mm(second, WU[:, cols])
+            off = pl.multiple_of(t * U, 128)
+            off2 = pl.multiple_of(2 * t * U, 128)
+            ab = mm(L[l, N2, m], WGU[:, pl.ds(off2, 2 * U)])
+            a, b = ab[:, 0:U], ab[:, U : 2 * U]
             sig = jax.nn.sigmoid(a)
             silu = a * sig
             R[l, m, :, pl.ds(CS + off, U)] = (silu * b).astype(bf16)
             if l == 0:
-                R[l, m, :, pl.ds(CA + off, U)] = a.astype(bf16)
-                R[l, m, :, pl.ds(CB + off, U)] = b.astype(bf16)
+                R[l, m, :, pl.ds(CA + off2, 2 * U)] = ab.astype(bf16)
             else:
-                ds = mm(L[l, DF, m], WD[pl.ds(off, U), :], NT)
-                R[l, m, :, pl.ds(CA + off, U)] = (ds * b * sig * (1.0 + a * (1.0 - sig))).astype(bf16)
-                R[l, m, :, pl.ds(CB + off, U)] = (ds * silu).astype(bf16)
-
-        ffn_tiles(body, low, high)
+                ds = R[l, m, :, pl.ds(CA + U + off2, U)].astype(f32)
+                R[l, m, :, pl.ds(CA + off2, U)] = (ds * b * sig * (1.0 + a * (1.0 - sig))).astype(bf16)
+                R[l, m, :, pl.ds(CA + U + off2, U)] = (ds * silu).astype(bf16)
+            return 0
+
+        lax.fori_loop(0, F // U, step, 0)
 
     def ffn_down(l, m):
-        act = R[l, m, :, CS : CS + F]
-        put_partial(m, lambda cols: mm(act, WD[:, cols]))
+        put_partial(m, lambda cols: mm(R[l, m, :, CS : CS + F], WD[:, cols]))
 
     def ffn_bwd(l, m):
         if l == 0:
-            def body(off):
-                a = R[l, m, :, pl.ds(CA + off, U)].astype(f32)
-                b = R[l, m, :, pl.ds(CB + off, U)].astype(f32)
+            def step(t, _):
+                off = pl.multiple_of(t * U, 128)
+                off2 = pl.multiple_of(2 * t * U, 128)
+                a = R[l, m, :, pl.ds(CA + off2, U)].astype(f32)
+                b = R[l, m, :, pl.ds(CA + U + off2, U)].astype(f32)
                 sig = jax.nn.sigmoid(a)
                 ds = mm(L[l, DF, m], WD[pl.ds(off, U), :], NT)
-                R[l, m, :, pl.ds(CA + off, U)] = (ds * b * sig * (1.0 + a * (1.0 - sig))).astype(bf16)
-                R[l, m, :, pl.ds(CB + off, U)] = (ds * a * sig).astype(bf16)
-
-            ffn_tiles(body)
-        da = R[l, m, :, CA : CA + F]
-        db = R[l, m, :, CB : CB + F]
-        put_partial(m, lambda cols: mm(da, WG[cols, :], NT) + mm(db, WU[cols, :], NT))
+                R[l, m, :, pl.ds(CA + off2, U)] = (ds * b * sig * (1.0 + a * (1.0 - sig))).astype(bf16)
+                R[l, m, :, pl.ds(CA + U + off2, U)] = (ds * a * sig).astype(bf16)
+                return 0
+
+            lax.fori_loop(0, F // U, step, 0)
+        put_partial(m, lambda cols: mm(R[l, m, :, CA : CA + 2 * F], WGU[cols, :], NT))
 
     def conv_bwd_a(l, m):
-        dz = mm(L[l, DO, m], WOUT[l], NT)
+        dz = mm(L[l, DO, m], WOUT[...], NT)
         bgate = R[l, m, :, CP : CP + C].astype(f32)
         xin = R[l, m, :, CP + 2 * C : CP + 3 * C].astype(f32)
         EXT[8 : 8 + TOK] = (bgate * xin).astype(bf16).astype(f32)
@@ -557,8 +629,7 @@
         xin = R[l, m, :, CP + 2 * C : CP + 3 * C].astype(f32)
         R[l, m, :, CP : CP + C] = (dbx * xin).astype(bf16)
         R[l, m, :, CP + 2 * C : CP + 3 * C] = (dbx * bgate).astype(bf16)
-        dp = R[l, m, :, CP : CP + 3 * C]
-        put_partial(m, lambda cols: mm(dp, WIN[l, cols, :], NT))
+        put_partial(m, lambda cols: mm(R[l, m, :, CP : CP + 3 * C], WIN[cols, :], NT))
 
     lanes = ((GA, (RA0, RA1, RA2)), (GB, (RB0, RB1, RB2)))
 
@@ -595,16 +666,16 @@
                 RT[0:wide, m * TOK : (m + 1) * TOK] = R[l, m, :, pl.ds(start, wide)].T
 
             def step(j, _):
-                src = L[l, kind, :, :, pl.ds(pl.multiple_of(j * 256, 256), 256)].reshape(M * TOK, 256)
+                src = L[l, kind, :, :, pl.ds(pl.multiple_of(j * 512, 512), 512)].reshape(M * TOK, 512)
                 res = mm(RT[0:wide], src).astype(bf16)
-                hi, lo = lax.div(j, 2), lax.rem(j, 2)
-                for y in range(2):
-                    block = res[:, y * 128 : (y + 1) * 128]
-                    GA[slot, y * 4 + lo * 2 + hi, 0:cut] = block[:cut]
-                    GB[slot, lo * 4 + hi * 2 + y, 0 : wide - cut] = block[cut:]
+                for q in range(4):
+                    lo, y = q // 2, q % 2
+                    block = res[:, q * 128 : (q + 1) * 128]
+                    GA[slot, y * 4 + lo * 2 + j, 0:cut] = block[:cut]
+                    GB[slot, lo * 4 + j * 2 + y, 0 : wide - cut] = block[cut:]
                 return 0
 
-            lax.fori_loop(0, D // 256, step, 0)
+            lax.fori_loop(0, D // 512, step, 0)
             for lane in range(2):
                 rs_copy(lane, 0, t, rows).start()
 
@@ -639,12 +710,14 @@
         def at(first):
             return pl.ds((v - first) * U if isinstance(v, int) else pl.multiple_of((v - first) * U, 128), U)
 
+        pair = div(v - fu, 2) * U
+        tile = pl.ds(pair if isinstance(v, int) else pl.multiple_of(pair, 128), U)
         if which == 0:
             pairs = [(FO, out_down.at[l, at(0)])]
         elif which == 1:
-            pairs = [(FT, out_gate.at[l, :, at(fu)])]
+            pairs = [(FT, out_gate.at[l, :, tile])]
         elif which == 2:
-            pairs = [(FT, out_up.at[l, :, at(2 * fu)])]
+            pairs = [(FT, out_up.at[l, :, tile])]
         elif which == 3:
             pairs = [(FT.at[:, pl.ds(0, C)], out_in.at[l, 0]),
                      (FT.at[:, pl.ds(C, U - C)], out_in.at[l, 1, :, pl.ds(0, U - C)])]
@@ -656,9 +729,15 @@
         return [pltpu.make_async_copy(a, b, fos.at[i]) for i, (a, b) in enumerate(pairs)]
 
     def by_target(t, fn):
+        v = rem(t, PER)
         fu = F // U
-        edges = (0, fu, 2 * fu, 3 * fu, 3 * fu + 1, 3 * fu + 2, PER)
-        cases(rem(t, PER), [(edges[i], edges[i + 1], functools.partial(fn, i)) for i in range(6)])
+        if isinstance(v, int):
+            fn(0 if v < fu else 1 + (v - fu) % 2 if v < 3 * fu else 3 + v - 3 * fu)
+            return
+        cases(v, [(0, fu, functools.partial(fn, 0))])
+        for i in range(2):
+            pl.when((v >= fu) & (v < 3 * fu) & (lax.rem(v + fu, 2) == i))(functools.partial(fn, 1 + i))
+        cases(v, [(3 * fu + i, 3 * fu + i + 1, functools.partial(fn, 3 + i)) for i in range(3)])
 
     def unit_wait(t):
         def go(which):
@@ -738,40 +817,73 @@
 
     end_o0 = functools.partial(finish_norm, 0, 1, N2)
     end_f0 = functools.partial(finish_norm, 1, 0, N1)
-    end_o1 = functools.partial(finish_norm, 1, 1, N2)
+    end_o1 = functools.partial(finish_norm, 1, 1, N2, within=True)
     end_n1 = functools.partial(finish_dn2, 1)
     end_c1 = functools.partial(finish_dn1, 1)
     end_n0 = functools.partial(finish_dn2, 0)
     end_c0 = functools.partial(finish_dn1, 0)
 
     arrived(load_conv(0))
-    phase(None, end_o0, lambda m: conv_fwd_a(0, m), lambda m: conv_fwd_b(0, m))
+    for cp in [load_og, load_down(1)] + load_ffn(0):
+        cp.start()
+
+    conv_fwd_a(0, jnp.int32(0))
+
+    def o0(m, _):
+        conv_fwd_b(0, m)
+        pl.when(m < M - 1)(lambda: conv_fwd_a(0, m + 1))
+        behind(None, end_o0, m)
+        gather_dyn(0, m, 0)
+
+        @pl.when(m == 0)
+        def _():
+            arrived([load_og, load_down(1)])
+
+        down_back(m)
+        gather_dyn(0, m, 1)
+        return 0
+
+    lax.fori_loop(0, M, o0, 0)
+    for cp in [load_down(0)] + load_conv(1):
+        cp.start()
     arrived(load_ffn(0))
 
-    def f0(m):
+    def f0(m, _):
         agcopy(0, N2, m).wait()
         ffn_fwd(0, m)
+        pl.when(m == 0)(lambda: load_down(0).wait())
         ffn_down(0, m)
-
-    phase(end_o0, end_f0, f0)
+        gather_dyn(2 * M, m, 0)
+        behind(end_o0, end_f0, m)
+        gather_dyn(2 * M, m, 1)
+
+        @pl.when(m == M - 1)
+        def _():
+            arrived(load_conv(1) + [tap_copy])
+            conv_fwd_a(1, 0)
+
+        return 0
+
+    lax.fori_loop(0, M, f0, 0)
     for cp in load_ffn(1):
         cp.start()
-    arrived(load_conv(1))
-    phase(end_f0, end_o1, lambda m: conv_fwd_a(1, m), lambda m: conv_fwd_b(1, m))
-    arrived(load_ffn(1) + [load_og])
-
-    agcopy(1, N2, 0).wait()
-    ffn_fwd(1, 0)
-    mid(M - 1)
-    end_o1(M - 2)
-    agcopy(1, N2, 1).wait()
-    ffn_fwd(1, 1)
-    agcopy(1, N2, 2).wait()
-    ffn_fwd(1, 2, 0, 2)
-    end_o1(M - 1)
-    ffn_fwd(1, 2, 2)
-    agcopy(1, N2, 3).wait()
-    ffn_fwd(1, 3)
+
+    def ffn_both(m):
+        agcopy(1, N2, m).wait()
+        ffn_fwd(1, m)
+
+    def o1(m, _):
+        pl.when(m == 0)(lambda: mid(M - 1))
+        conv_fwd_b(1, m)
+        pl.when(m < M - 1)(lambda: conv_fwd_a(1, m + 1))
+        end_o1(m)
+        pl.when(m == 1)(lambda: arrived(load_ffn(1)))
+        pl.when(m >= 1)(lambda: ffn_both(m - 1))
+        pl.when(m < 2)(lambda: end_f0(m + 2))
+        return 0
+
+    lax.fori_loop(0, M, o1, 0)
+    ffn_both(M - 1)
     tick_gen(0)
 
     def start_c1(m):
@@ -788,6 +900,8 @@
     for cp in load_ffn(0):
         cp.start()
     phase(end_n1, end_c1, None, lambda m: conv_bwd_b(1, m), tick=1 + M, ahead=next_one(start_c1))
+    for cp in load_conv(0):
+        cp.start()
     arrived(load_ffn(0))
 
     def n0(m):
@@ -809,8 +923,9 @@
         return 0
 
     lax.fori_loop(0, M, n0_tick, 0)
-    load_ffn(1)[2].start()
-    load_ffn(1)[2].wait()
+    load_down(1).start()
+    load_down(1).wait()
+    arrived(load_conv(0))
 
     def f1(m):
         agcopy(0, DO, m).wait()
@@ -906,10 +1021,9 @@
         scratch_shapes=[
             vm((LAYERS, 4, M, TOK, D), bf16),
             vm((LAYERS, M, TOK, 3 * F + 4 * C), bf16),
-            vm((LAYERS, D, 3 * C), bf16),
-            vm((LAYERS, C, D), bf16),
-            vm((D, F), bf16),
-            vm((D, F), bf16),
+            vm((D, 3 * C), bf16),
+            vm((C, D), bf16),
+            vm((D, 2 * F), bf16),
             vm((F, D), bf16),
             vm((M, half, D), f32),
             vm((M, half, D), f32),
@@ -931,16 +1045,19 @@
             vm((8, D), f32),
             vm((TOK + 8, C), f32),
             vm((2, TOK + 8, C), f32),
+            vm((TOK, C), f32),
             vm((LAYERS, M, 8, C), f32),
+            vm((M, 8, C), f32),
             vm((LAYERS, M, 8, C), f32),
             vm((4, LAYERS, D), f32),
+            vm((3, LAYERS, C), f32),
             vm((3, LAYERS, C), f32),
             vm((4, 8, D), f32),
             vm((LAYERS, 3, 8, C), f32),
             vm((4, 8, D), f32),
             dma((16,)),
             dma((M,)), dma((M,)), dma((M,)), dma((M,)), dma((M,)), dma((M,)),
-            dma, dma((2,)), dma((2, LAYERS, M)),
+            dma, dma((2,)), dma((2, LAYERS, M)), dma((2,)), dma((M + 1,)), dma((4, 5)), dma((4, 5)),
             dma((2, 3, S)), dma((2, 3, S)),
             dma((2,)), dma((M,)), dma((M,)), dma((M,)), dma((4,)), dma((4,)),
         ],
@@ -951,13 +1068,45 @@
     )(stream_in, norm_gain, win, taps, wout, ffn_gain, wgate, wup, wdown, out_grad)
 
 
+def handed_on(*refs):
+    count = (len(refs) - 2) // 3
+    srcs, dsts, bufs = refs[:count], refs[count : 2 * count], refs[2 * count : 3 * count]
+    sin, sout = refs[-2:]
+    chunks = [(i, k) for i in range(count) for k in range(srcs[i].shape[0])]
+    ins = [pltpu.make_async_copy(srcs[i].at[k], bufs[i].at[k], sin.at[i, k]) for i, k in chunks]
+    outs = [pltpu.make_async_copy(bufs[i].at[k], dsts[i].at[k], sout.at[i, k]) for i, k in chunks]
+    for cp in ins:
+        cp.start()
+    for first, second in zip(ins, outs):
+        first.wait()
+        second.start()
+    for cp in outs:
+        cp.wait()
+
+
+def hand_on(arrays):
+    anys = pl.BlockSpec(memory_space=pl.ANY)
+    most = max(a.shape[0] for a in arrays)
+    return pl.pallas_call(
+        handed_on,
+        out_shape=[jax.ShapeDtypeStruct(a.shape, a.dtype) for a in arrays],
+        in_specs=[anys] * len(arrays),
+        out_specs=[anys] * len(arrays),
+        scratch_shapes=[pltpu.VMEM(a.shape, a.dtype) for a in arrays]
+        + [pltpu.SemaphoreType.DMA((len(arrays), most))] * 2,
+        name="hand_on",
+        compiler_params=pltpu.CompilerParams(vmem_limit_bytes=VMEM_BYTES),
+    )(*arrays)
+
+
 def body_fused(
     stream_in, norm_gain, in_proj, conv_taps, out_proj, ffn_gain, gate_proj, up_proj, down_proj, out_grad
 ):
-    (out_stream, out_sgrad, norm_g, in_g, conv_g, out_g, ffn_g, gate_g, up_g, down_g) = fused_call(
+    results = fused_call(
         stream_in, norm_gain, jnp.transpose(in_proj, (0, 2, 1, 3)), jnp.transpose(conv_taps, (1, 0, 2)),
         out_proj, ffn_gain, gate_proj, up_proj, down_proj, out_grad,
     )
+    (out_stream, out_sgrad, norm_g, in_g, conv_g, out_g, ffn_g, gate_g, up_g, down_g) = hand_on(results)
     in_g = jnp.transpose(in_g, (0, 2, 1, 3))
     conv_g = jnp.transpose(conv_g, (1, 0, 2))
     return (out_stream, out_sgrad, norm_g, in_g, conv_g, out_g, ffn_g, gate_g, up_g, down_g)

time: 297 us -> 287 us (0.966)
  local copies, waits for them, and re-layouts: 11.7 us -> 0 us
    unnamed x28 -> x0, local copies, waits for them, and re-layouts: 11.7 us -> none
    pallas_call x0 -> x1, Pallas kernels: none -> 8.92 us  [hand_on(): pl.pallas_call(handed_on, out_shape=[jax.ShapeDtypeStruct(a.shape, a.dtyp...]
    pallas_call x1, Pallas kernels: 285 us -> 277 us  [fused_call(): pl.pallas_call(functools.partial(fused, (M, TOK, D, C, F, U)), out_shape=...]
where the time goes in v3:
time: 287 us
  Pallas kernels  286 us (100%)
    pallas_call x1, Pallas kernels, fused_call(): pl.pallas_call(functools.partial(fused, (M, TOK, D, C, F, U)), out_shape=...  277 us
    pallas_call x1, Pallas kernels, hand_on(): pl.pallas_call(handed_on, out_shape=[jax.ShapeDtypeStruct(a.shape, a.dtyp...  8.92 us

profile of v3, /device:TPU:0, one launch (start us, length us, event | category | flops | bytes accessed | tf_op | source)
XLA Modules:
  0.0 287.2 jit_solution(9550361667364235981)
XLA Ops:
  0.6 277.4 %fused.1 = (bf16[4,256,1024]{2,1,0:T(8,128)(2,1)}, f32[4,256,1024]{2,1,0:T(8,128)}, f32[2,256]{1,0:T(2,128)}, f32[2,3,128,256]{3,2,1,0:T(8,128)}, f32[3,2,256]{2...) custom-call(bf16[4,256,1024]{2,1,0:T(8,128)(2,1)} %stream_in.1, ...), custom_call_target="tpu_custom_call" | custom-call | tf_op jit(solution)/shard_map/fused/pallas_call | solution.py:1005
  278.1 8.9 %hand_on.1 = (bf16[4,256,1024]{2,1,0:T(8,128)(2,1)}, f32[4,256,1024]{2,1,0:T(8,128)}, f32[2,256]{1,0:T(2,128)}, f32[2,3,128,256]{3,2,1,0:T(8,128)}, f32[3,2,256]...) custom-call(bf16[4,256,1024]{2,1,0:T(8,128)(2,1)} %get-tuple-element, ...), custom_call_target="tpu_custom_call" | custom-call | tf_op jit(solution)/shard_map/hand_on/pallas_call | solution.py:1090

commit v4 on v3

--- a/solution.py
+++ b/solution.py
@@ -219,7 +219,7 @@
 bf16 = jnp.bfloat16
 NN = (((1,), (0,)), ((), ()))
 NT = (((1,), (1,)), ((), ()))
-ORDERS = ((0, 1, 2), (1, 2, 0))
+ORDERS = ((0, 1, 2), (1, 0, 2))
 SLOTS = 4
 WIDE = 512
 N1, N2, DF, DO = range(4)
@@ -253,17 +253,20 @@
     L, R, WIN, WOUT, WGU, WD, H, DH, RATE, PB, PR, XR,
     GA, GB, RA0, RA1, RA2, RB0, RB1, RB2, RT, FO, FT, SM,
     EXT, DYE, CF, HALO, HALO2, DHALO, GAIN, TAPS, TAPS2, GACC, CACC, SMR,
+    GAIN_IN, FGAIN_IN, TAPS_IN, NORM_OUT, FFN_OUT, CONV_OUT,
     load_sem, ps, pr, xs, xr, ags, agr, hs, dhs, hr, hs2, hr2, gs, gr, rss, rsr, fos, oss, sts, str_, sms, smr,
 ):
     M, TOK, D, C, F, U = dims
     half = TOK // 2
     CS, CA, CP, CZ = 0, F, 3 * F, 3 * F + 3 * C
-    UNITS = 2 * (-(-(CZ + C) // U))
-    PER = UNITS // 2
-    full = (U, GA.shape[2], GB.shape[2])
-    width = CZ + C - (PER - 1) * U
-    tail_b = width // 6 // 16 * 16 + 16 * (width % 96 > 0)
-    short = (width, width - tail_b, tail_b)
+    PER = (CZ + C) // U
+    first_units = [(1, 0, 128), (1, 128, U - 128)]
+    TURN = PER + 2
+    table = first_units + [(1, k * U, U) for k in range(1, PER)] + [(1, PER * U, CZ + C - PER * U)]
+    table += [(0, k * U, U) for k in range(PER)]
+    table += [(0, k, 128) for k in range(PER * U, CZ + C, 128)]
+    UNITS = len(table)
+    splits = {w: (w, w - w // 4, w // 4) for w in (128, 256, U)}
     seq = lax.axis_index("seq")
     tp = lax.axis_index("tp")
     n = lax.axis_size("seq")
@@ -313,11 +316,19 @@
     for dev in others:
         pl.semaphore_signal(barrier, inc=1, device_id=dev, device_id_type=MESH)
 
-    GAIN[0] = norm_gain[...].astype(f32)
-    GAIN[1] = ffn_gain[...].astype(f32)
-    GAIN[2] = 1.0 / norm_gain[...].astype(f32)
-    GAIN[3] = 1.0 / ffn_gain[...].astype(f32)
-    TAPS[...] = taps[...].astype(f32)
+    small_in = [
+        pltpu.make_async_copy(src, dst, load_sem.at[16 + i])
+        for i, (src, dst) in enumerate(((norm_gain, GAIN_IN), (ffn_gain, FGAIN_IN), (taps, TAPS_IN)))
+    ]
+    for cp in small_in:
+        cp.start()
+    for cp in small_in:
+        cp.wait()
+    GAIN[0] = GAIN_IN[...].astype(f32)
+    GAIN[1] = FGAIN_IN[...].astype(f32)
+    GAIN[2] = 1.0 / GAIN_IN[...].astype(f32)
+    GAIN[3] = 1.0 / FGAIN_IN[...].astype(f32)
+    TAPS[...] = TAPS_IN[...].astype(f32)
     GACC[...] = jnp.zeros_like(GACC)
     CACC[...] = jnp.zeros_like(CACC)
 
@@ -467,9 +478,11 @@
     def finish_dn1(l, m):
         def emit(loc, rows, delta):
             new = DH[m, loc] + delta
-            DH[m, loc] = new
             if l == 1:
+                DH[m, loc] = new
                 L[0, DF, m, rows] = new.astype(bf16)
+            else:
+                PB[m, rows] = new.astype(bf16)
 
         norm_back(l, 0, N1, m, emit)
         if l == 1:
@@ -480,8 +493,8 @@
 
     def grad_copies(m):
         return (
-            pltpu.make_async_copy(DH.at[m], out_sgrad.at[m, mine], oss.at[m]),
-            remote(DH.at[m], out_sgrad.at[m, mine], ags.at[m], agr.at[m], sib),
+            pltpu.make_async_copy(PB.at[m, mine], out_sgrad.at[m, mine], oss.at[m]),
+            remote(PB.at[m, mine], out_sgrad.at[m, mine], ags.at[m], agr.at[m], sib),
         )
 
     def put_partial(m, tile):
@@ -493,8 +506,11 @@
         lax.fori_loop(0, D // WIDE, step, 0)
         pcopy(m).start()
 
+    def halo_rows(m):
+        return pl.ds(m * 8 if isinstance(m, int) else pl.multiple_of(m * 8, 8), 8)
+
     def hcopy(l, m):
-        return remote(EXT.at[pl.ds(TOK, 8)], HALO.at[l, m], hs, hr.at[0, l, m], nxt)
+        return remote(EXT.at[pl.ds(TOK, 8)], HALO.at[l, halo_rows(m)], hs, hr.at[0, l, m], nxt)
 
     def dhcopy(l, m):
         return remote(DYE.at[rem(m, 2), pl.ds(0, 8)], DHALO.at[l, m], dhs.at[rem(m, 2)], hr.at[1, l, m], prv)
@@ -511,15 +527,24 @@
         return t[0] * ext[6 : 6 + TOK] + t[1] * ext[7 : 7 + TOK] + t[2] * ext[8 : 8 + TOK]
 
     def conv_now(l, m):
-        return conv_of(EXT, HALO[l, m], TAPS, l)
+        return conv_of(EXT, HALO[l, halo_rows(m)], TAPS, l)
 
     def other_in(k):
         blocks = [L[0, DO, 1 + k, :, r * TOK : (r + 1) * TOK] for r in range(D // TOK)]
         return jnp.concatenate(blocks, axis=0)
 
+    first_halos = remote(DYE.at[1, pl.ds(0, 8 * M)], HALO.at[0], hs, hr.at[0, 0, 0], nxt)
+
+    def send_first_halos():
+        val = jnp.concatenate([L[0, N1, m, TOK - 16 : TOK] for m in range(M)], axis=0).astype(f32)
+        p = mm((val * rate_of(val) * GAIN[0, 0:1, :]).astype(bf16), WIN[...])
+        bx = (p[:, 0:C] * p[:, 2 * C : 3 * C]).astype(bf16).astype(f32)
+        for m in range(M):
+            DYE[1, 8 * m : 8 * m + 8] = bx[16 * m + 8 : 16 * m + 16]
+        first_halos.start()
+
     def conv_fwd_a(l, m):
         if l == 0:
-            load_stream(m).wait()
             gain = GAIN[0, 0:1, :]
             hid = L[0, N1, m, mine].astype(f32)
             H[m] = hid
@@ -539,16 +564,19 @@
         bgate, cgate, xin = p[:, 0:C], p[:, C : 2 * C], p[:, 2 * C : 3 * C]
         R[l, m, :, CP : CP + 3 * C] = p.astype(bf16)
         EXT[8 : 8 + TOK] = (bgate * xin).astype(bf16).astype(f32)
-        hcopy(l, m).start()
         DYE[0, 0:TOK] = cgate
         if l == 1:
+            hcopy(l, m).start()
             p = mm(first, jnp.concatenate([other_in(k) for k in range(3)], axis=1))
             DYE[1, 8 : 8 + TOK] = (p[:, 0:C] * p[:, 2 * C : 3 * C]).astype(bf16).astype(f32)
             hcopy2(m).start()
             CF[...] = p[:, C : 2 * C]
 
     def conv_fwd_b(l, m):
-        hcopy(l, m).wait()
+        if l == 0:
+            pl.when(m == 0)(lambda: first_halos.wait())
+        else:
+            hcopy(l, m).wait()
         gated = (DYE[0, 0:TOK] * conv_now(l, m)).astype(bf16)
         R[l, m, :, CZ : CZ + C] = gated
         if l == 0:
@@ -567,7 +595,7 @@
         for t in range(F // U):
             R[1, m, :, CA + (2 * t + 1) * U : CA + (2 * t + 2) * U] = ds[:, t * U : (t + 1) * U]
 
-    def ffn_fwd(l, m):
+    def ffn_fwd(l, m, low=0, high=F // U):
         def step(t, _):
             off = pl.multiple_of(t * U, 128)
             off2 = pl.multiple_of(2 * t * U, 128)
@@ -584,7 +612,7 @@
                 R[l, m, :, pl.ds(CA + U + off2, U)] = (ds * silu).astype(bf16)
             return 0
 
-        lax.fori_loop(0, F // U, step, 0)
+        lax.fori_loop(low, high, step, 0)
 
     def ffn_down(l, m):
         put_partial(m, lambda cols: mm(R[l, m, :, CS : CS + F], WD[:, cols]))
@@ -637,8 +665,19 @@
         b = [bits[o] for o in ORDERS[lane]]
         return [b[0] * 4, b[0] * 4 + b[1] * 2, b[0] * 4 + b[1] * 2 + b[2]][step]
 
+    def unit_at(t):
+        if isinstance(t, int):
+            return table[t][:2]
+        k = jnp.where(t < TURN, t - 1, t - TURN)
+        return jnp.where(t < TURN, 1, 0), jnp.where(t < 2, t * 128, k * U)
+
     def sized(t, fn):
-        cases(rem(t, PER), [(0, PER - 1, lambda: fn(full)), (PER - 1, PER, lambda: fn(short))])
+        if isinstance(t, int):
+            fn(splits[table[t][2]])
+            return
+        pl.when(t == 0)(lambda: fn(splits[128]))
+        pl.when((t == 1) | (t == TURN - 1))(lambda: fn(splits[256]))
+        pl.when((t > 1) & (t != TURN - 1))(lambda: fn(splits[U]))
 
     def rs_copy(lane, step, t, rows):
         G, recv = lanes[lane]
@@ -653,17 +692,15 @@
         )
 
     def rs_gen(t):
-        l = 1 - div(t, PER)
-        v = rem(t, PER)
-        fu = F // U
-        kind = jnp.where(v < fu, DF, jnp.where(v < 3 * fu, N2, jnp.where(v < PER - 1, N1, DO)))
+        l, start = unit_at(t)
+        kind = jnp.where(start < CA, DF, jnp.where(start < CP, N2, jnp.where(start < CZ, N1, DO)))
         slot = rem(t, SLOTS)
 
         def make(rows):
             wide, cut, _ = rows
-            start = v * U if isinstance(v, int) else pl.multiple_of(v * U, 128)
+            cols = pl.ds(start if isinstance(start, int) else pl.multiple_of(start, 128), wide)
             for m in range(M):
-                RT[0:wide, m * TOK : (m + 1) * TOK] = R[l, m, :, pl.ds(start, wide)].T
+                RT[0:wide, m * TOK : (m + 1) * TOK] = R[l, m, :, cols].T
 
             def step(j, _):
                 src = L[l, kind, :, :, pl.ds(pl.multiple_of(j * 512, 512), 512)].reshape(M * TOK, 512)
@@ -672,7 +709,7 @@
                     lo, y = q // 2, q % 2
                     block = res[:, q * 128 : (q + 1) * 128]
                     GA[slot, y * 4 + lo * 2 + j, 0:cut] = block[:cut]
-                    GB[slot, lo * 4 + j * 2 + y, 0 : wide - cut] = block[cut:]
+                    GB[slot, lo * 4 + y * 2 + j, 0 : wide - cut] = block[cut:]
                 return 0
 
             lax.fori_loop(0, D // 512, step, 0)
@@ -702,18 +739,15 @@
 
         sized(t, go)
 
-    def unit_copies(t, which):
-        l = 1 - div(t, PER)
-        v = rem(t, PER)
-        fu = F // U
-
-        def at(first):
-            return pl.ds((v - first) * U if isinstance(v, int) else pl.multiple_of((v - first) * U, 128), U)
-
-        pair = div(v - fu, 2) * U
-        tile = pl.ds(pair if isinstance(v, int) else pl.multiple_of(pair, 128), U)
+    def unit_copies(t, which, wide):
+        l, start = unit_at(t)
+
+        def at(off):
+            return pl.ds(off if isinstance(off, int) else pl.multiple_of(off, 128), wide)
+
+        tile = at(div(start - CA, 2 * U) * U)
         if which == 0:
-            pairs = [(FO, out_down.at[l, at(0)])]
+            pairs = [(FO.at[pl.ds(0, wide)], out_down.at[l, at(start)])]
         elif which == 1:
             pairs = [(FT, out_gate.at[l, :, tile])]
         elif which == 2:
@@ -725,23 +759,33 @@
             pairs = [(FT.at[:, pl.ds(0, 2 * C - U)], out_in.at[l, 1, :, pl.ds(U - C, 2 * C - U)]),
                      (FT.at[:, pl.ds(2 * C - U, C)], out_in.at[l, 2])]
         else:
-            pairs = [(FO.at[pl.ds(0, width)], out_out.at[l])]
+            pairs = [(FO.at[pl.ds(0, wide)], out_out.at[l, at(start - CZ)])]
         return [pltpu.make_async_copy(a, b, fos.at[i]) for i, (a, b) in enumerate(pairs)]
 
     def by_target(t, fn):
-        v = rem(t, PER)
-        fu = F // U
-        if isinstance(v, int):
-            fn(0 if v < fu else 1 + (v - fu) % 2 if v < 3 * fu else 3 + v - 3 * fu)
+        if isinstance(t, int):
+            _, start, wide = table[t]
+            if start < CA:
+                which = 0
+            elif start < CP:
+                which = 1 + (start - CA) // U % 2
+            else:
+                which = 5 if start >= CZ else 3 + (start - CP) // U
+            fn(which, wide)
             return
-        cases(v, [(0, fu, functools.partial(fn, 0))])
+        _, start = unit_at(t)
+        pl.when(t == 0)(lambda: fn(0, 128))
+        pl.when(t == 1)(lambda: fn(0, 256))
+        pl.when((t > 1) & (start < CA))(lambda: fn(0, U))
         for i in range(2):
-            pl.when((v >= fu) & (v < 3 * fu) & (lax.rem(v + fu, 2) == i))(functools.partial(fn, 1 + i))
-        cases(v, [(3 * fu + i, 3 * fu + i + 1, functools.partial(fn, 3 + i)) for i in range(3)])
+            odd = lax.rem(lax.div(start, U) + CA // U, 2) == i
+            pl.when((start >= CA) & (start < CP) & odd)(functools.partial(fn, 1 + i, U))
+            pl.when(start == CP + i * U)(functools.partial(fn, 3 + i, U))
+        pl.when(start == CZ)(lambda: fn(5, 256))
 
     def unit_wait(t):
-        def go(which):
-            for cp in unit_copies(t, which):
+        def go(which, wide):
+            for cp in unit_copies(t, which, wide):
                 cp.wait()
 
         by_target(t, go)
@@ -758,17 +802,17 @@
             wide, cut, _ = rows
             for lane in range(2):
                 rs_copy(lane, 2, t, rows).wait()
-            FO[0:cut] = GA[slot, keep(0, 2), 0:cut].astype(f32) + RA2[slot, 0, 0:cut].astype(f32)
+            FO[0:cut] = (GA[slot, keep(0, 2), 0:cut].astype(f32) + RA2[slot, 0, 0:cut].astype(f32)).astype(bf16)
             FO[cut:wide] = (
                 GB[slot, keep(1, 2), 0 : wide - cut].astype(f32) + RB2[slot, 0, 0 : wide - cut].astype(f32)
-            )
+            ).astype(bf16)
 
         sized(t, go)
 
-        def send(which):
+        def send(which, wide):
             if which in (1, 2, 3, 4):
                 FT[...] = FO[...].T
-            for cp in unit_copies(t, which):
+            for cp in unit_copies(t, which, wide):
                 cp.start()
 
         by_target(t, send)
@@ -823,7 +867,8 @@
     end_n0 = functools.partial(finish_dn2, 0)
     end_c0 = functools.partial(finish_dn1, 0)
 
-    arrived(load_conv(0))
+    arrived(load_conv(0) + [load_stream(m) for m in range(M)])
+    send_first_halos()
     for cp in [load_og, load_down(1)] + load_ffn(0):
         cp.start()
 
@@ -854,14 +899,16 @@
         pl.when(m == 0)(lambda: load_down(0).wait())
         ffn_down(0, m)
         gather_dyn(2 * M, m, 0)
-        behind(end_o0, end_f0, m)
-        gather_dyn(2 * M, m, 1)
+        mid(lax.rem(m + M - 1, M))
 
         @pl.when(m == M - 1)
         def _():
             arrived(load_conv(1) + [tap_copy])
             conv_fwd_a(1, 0)
 
+        pl.when(m < 2)(lambda: end_o0(m + M - 2))
+        pl.when(m >= 2)(lambda: end_f0(m - 2))
+        gather_dyn(2 * M, m, 1)
         return 0
 
     lax.fori_loop(0, M, f0, 0)
@@ -883,8 +930,10 @@
         return 0
 
     lax.fori_loop(0, M, o1, 0)
-    ffn_both(M - 1)
+    agcopy(1, N2, M - 1).wait()
+    ffn_fwd(1, M - 1, 0, 1)
     tick_gen(0)
+    ffn_fwd(1, M - 1, 1)
 
     def start_c1(m):
         agcopy(1, DO, m).wait()
@@ -974,17 +1023,25 @@
             small(i + 1).start()
         tick_rest(t)
         t += 1
+    own = pl.ds(pl.multiple_of(tp * C, 128), C)
+    NORM_OUT[...] = SM[0:2, own]
+    FFN_OUT[...] = SM[2:4, own]
+    for l in range(2):
+        for k in range(3):
+            CONV_OUT[k, l : l + 1, :] = SM[4 + l : 5 + l, k * C : (k + 1) * C]
+    small_out = [
+        pltpu.make_async_copy(src, dst, load_sem.at[16 + i])
+        for i, (src, dst) in enumerate(((NORM_OUT, out_norm), (FFN_OUT, out_ffn), (CONV_OUT, out_conv)))
+    ]
+    for cp in small_out:
+        cp.start()
     while t < UNITS + 3:
         tick_gen(t)
         tick_rest(t)
         t += 1
-    own = pl.ds(pl.multiple_of(tp * C, 128), C)
-    out_norm[...] = SM[0:2, own]
-    out_ffn[...] = SM[2:4, own]
-    for l in range(2):
-        for k in range(3):
-            out_conv[k, l : l + 1, :] = SM[4 + l : 5 + l, k * C : (k + 1) * C]
     unit_wait(UNITS - 1)
+    for cp in small_out:
+        cp.wait()
     for m in range(M):
         for cp in grad_copies(m):
             cp.wait()
@@ -994,30 +1051,29 @@
     M, TOK, D = stream_in.shape
     C, F = wout.shape[1], wgate.shape[2]
     U = 384
-    rb = U // 6
+    rb = U // 4
     ra = U - rb
     half = TOK // 2
     vm = pltpu.VMEM
     dma = pltpu.SemaphoreType.DMA
     S = SLOTS
     anys = pl.BlockSpec(memory_space=pl.ANY)
-    vmem = pl.BlockSpec(memory_space=pltpu.VMEM)
     return pl.pallas_call(
         functools.partial(fused, (M, TOK, D, C, F, U)),
         out_shape=[
             jax.ShapeDtypeStruct((M, TOK, D), bf16),
-            jax.ShapeDtypeStruct((M, TOK, D), f32),
+            jax.ShapeDtypeStruct((M, TOK, D), bf16),
             jax.ShapeDtypeStruct((LAYERS, C), f32),
-            jax.ShapeDtypeStruct((LAYERS, 3, 128, C), f32),
+            jax.ShapeDtypeStruct((LAYERS, 3, 128, C), bf16),
             jax.ShapeDtypeStruct((3, LAYERS, C), f32),
-            jax.ShapeDtypeStruct((LAYERS, C, 128), f32),
+            jax.ShapeDtypeStruct((LAYERS, C, 128), bf16),
             jax.ShapeDtypeStruct((LAYERS, C), f32),
-            jax.ShapeDtypeStruct((LAYERS, 128, F), f32),
-            jax.ShapeDtypeStruct((LAYERS, 128, F), f32),
-            jax.ShapeDtypeStruct((LAYERS, F, 128), f32),
+            jax.ShapeDtypeStruct((LAYERS, 128, F), bf16),
+            jax.ShapeDtypeStruct((LAYERS, 128, F), bf16),
+            jax.ShapeDtypeStruct((LAYERS, F, 128), bf16),
         ],
-        in_specs=[anys, vmem, anys, vmem, anys, vmem, anys, anys, anys, anys],
-        out_specs=[anys, anys, vmem, anys, vmem, anys, vmem, anys, anys, anys],
+        in_specs=[anys] * 10,
+        out_specs=[anys] * 10,
         scratch_shapes=[
             vm((LAYERS, 4, M, TOK, D), bf16),
             vm((LAYERS, M, TOK, 3 * F + 4 * C), bf16),
@@ -1040,13 +1096,13 @@
             vm((S, 2, rb, 128), bf16),
             vm((S, 1, rb, 128), bf16),
             vm((U, M * TOK), bf16),
-            vm((U, 128), f32),
-            vm((128, U), f32),
+            vm((U, 128), bf16),
+            vm((128, U), bf16),
             vm((8, D), f32),
             vm((TOK + 8, C), f32),
             vm((2, TOK + 8, C), f32),
             vm((TOK, C), f32),
-            vm((LAYERS, M, 8, C), f32),
+            vm((LAYERS, M * 8, C), f32),
             vm((M, 8, C), f32),
             vm((LAYERS, M, 8, C), f32),
             vm((4, LAYERS, D), f32),
@@ -1055,7 +1111,13 @@
             vm((4, 8, D), f32),
             vm((LAYERS, 3, 8, C), f32),
             vm((4, 8, D), f32),
-            dma((16,)),
+            vm((LAYERS, D), bf16),
+            vm((LAYERS, D), bf16),
+            vm((3, LAYERS, C), bf16),
+            vm((LAYERS, C), f32),
+            vm((LAYERS, C), f32),
+            vm((3, LAYERS, C), f32),
+            dma((19,)),
             dma((M,)), dma((M,)), dma((M,)), dma((M,)), dma((M,)), dma((M,)),
             dma, dma((2,)), dma((2, LAYERS, M)), dma((2,)), dma((M + 1,)), dma((4, 5)), dma((4, 5)),
             dma((2, 3, S)), dma((2, 3, S)),
@@ -1068,31 +1130,47 @@
     )(stream_in, norm_gain, win, taps, wout, ffn_gain, wgate, wup, wdown, out_grad)
 
 
-def handed_on(*refs):
-    count = (len(refs) - 2) // 3
-    srcs, dsts, bufs = refs[:count], refs[count : 2 * count], refs[2 * count : 3 * count]
+def handed_on(kinds, *refs):
+    count = len(kinds)
+    srcs, dsts, bufs, wides = (refs[k * count : (k + 1) * count] for k in range(4))
     sin, sout = refs[-2:]
     chunks = [(i, k) for i in range(count) for k in range(srcs[i].shape[0])]
     ins = [pltpu.make_async_copy(srcs[i].at[k], bufs[i].at[k], sin.at[i, k]) for i, k in chunks]
-    outs = [pltpu.make_async_copy(bufs[i].at[k], dsts[i].at[k], sout.at[i, k]) for i, k in chunks]
+    outs = [
+        pltpu.make_async_copy((wides if kinds[i] else bufs)[i].at[k], dsts[i].at[k], sout.at[i, k]) for i, k in chunks
+    ]
     for cp in ins:
         cp.start()
-    for first, second in zip(ins, outs):
+    for (i, k), first, second in zip(chunks, ins, outs):
         first.wait()
+        if kinds[i]:
+            ref, wide = bufs[i].at[k], wides[i].at[k]
+            rows = 64
+            lead = ref.shape[:-2]
+
+            def step(r, _):
+                cut = pl.ds(pl.multiple_of(lax.rem(r, ref.shape[-2] // rows) * rows, rows), rows)
+                at = (lax.div(r, ref.shape[-2] // rows), cut) if lead else (cut,)
+                wide[at] = ref[at].astype(f32)
+                return 0
+
+            lax.fori_loop(0, (lead[0] if lead else 1) * ref.shape[-2] // rows, step, 0)
         second.start()
     for cp in outs:
         cp.wait()
 
 
-def hand_on(arrays):
+def hand_on(arrays, types):
     anys = pl.BlockSpec(memory_space=pl.ANY)
     most = max(a.shape[0] for a in arrays)
+    kinds = tuple(a.dtype != t for a, t in zip(arrays, types))
     return pl.pallas_call(
-        handed_on,
-        out_shape=[jax.ShapeDtypeStruct(a.shape, a.dtype) for a in arrays],
+        functools.partial(handed_on, kinds),
+        out_shape=[jax.ShapeDtypeStruct(a.shape, t) for a, t in zip(arrays, types)],
         in_specs=[anys] * len(arrays),
         out_specs=[anys] * len(arrays),
         scratch_shapes=[pltpu.VMEM(a.shape, a.dtype) for a in arrays]
+        + [pltpu.VMEM(a.shape if k else (8, 128), f32) for a, k in zip(arrays, kinds)]
         + [pltpu.SemaphoreType.DMA((len(arrays), most))] * 2,
         name="hand_on",
         compiler_params=pltpu.CompilerParams(vmem_limit_bytes=VMEM_BYTES),
@@ -1106,7 +1184,9 @@
         stream_in, norm_gain, jnp.transpose(in_proj, (0, 2, 1, 3)), jnp.transpose(conv_taps, (1, 0, 2)),
         out_proj, ffn_gain, gate_proj, up_proj, down_proj, out_grad,
     )
-    (out_stream, out_sgrad, norm_g, in_g, conv_g, out_g, ffn_g, gate_g, up_g, down_g) = hand_on(results)
+    (out_stream, out_sgrad, norm_g, in_g, conv_g, out_g, ffn_g, gate_g, up_g, down_g) = hand_on(
+        results, [bf16] + [f32] * 9
+    )
     in_g = jnp.transpose(in_g, (0, 2, 1, 3))
     conv_g = jnp.transpose(conv_g, (1, 0, 2))
     return (out_stream, out_sgrad, norm_g, in_g, conv_g, out_g, ffn_g, gate_g, up_g, down_g)

time: 287 us -> 277 us (0.965)
  Pallas kernels: 286 us -> 276 us
    pallas_call x1, Pallas kernels: 277 us -> 270 us  [fused_call(): pl.pallas_call(functools.partial(fused, (M, TOK, D, C, F, U)), out_shape=...]
where the time goes in v4:
time: 277 us
  Pallas kernels  276 us (100%)
    pallas_call x1, Pallas kernels, fused_call(): pl.pallas_call(functools.partial(fused, (M, TOK, D, C, F, U)), out_shape=...  270 us
    pallas_call x1, Pallas kernels, hand_on(): pl.pallas_call(functools.partial(handed_on, kinds), out_shape=[jax.ShapeD...  6.79 us

profile of v4, /device:TPU:0, one launch (start us, length us, event | category | flops | bytes accessed | tf_op | source)
XLA Modules:
  0.0 277.2 jit_solution(8964804327529172788)
XLA Ops:
  0.6 269.6 %fused.1 = (bf16[4,256,1024]{2,1,0:T(8,128)(2,1)}, bf16[4,256,1024]{2,1,0:T(8,128)(2,1)}, f32[2,256]{1,0:T(2,128)}, bf16[2,3,128,256]{3,2,1,0:T(8,128)(2,1)}, f3...) custom-call(bf16[4,256,1024]{2,1,0:T(8,128)(2,1)} %stream_in.1, ...), custom_call_target="tpu_custom_call" | custom-call | tf_op jit(solution)/shard_map/fused/pallas_call | solution.py:1061
  270.2 6.8 %hand_on.1 = (bf16[4,256,1024]{2,1,0:T(8,128)(2,1)}, f32[4,256,1024]{2,1,0:T(8,128)}, f32[2,256]{1,0:T(2,128)}, f32[2,3,128,256]{3,2,1,0:T(8,128)}, f32[3,2,256]...) custom-call(bf16[4,256,1024]{2,1,0:T(8,128)(2,1)} %get-tuple-element, ...), custom_call_target="tpu_custom_call" | custom-call | tf_op jit(solution)/shard_map/hand_on/pallas_call | solution.py:1167

commit v5 on v4

--- a/solution.py
+++ b/solution.py
@@ -221,7 +221,7 @@
 NT = (((1,), (1,)), ((), ()))
 ORDERS = ((0, 1, 2), (1, 0, 2))
 SLOTS = 4
-WIDE = 512
+WIDE = 1024
 N1, N2, DF, DO = range(4)
 
 
@@ -397,7 +397,7 @@
             PB[m, rows] = got.astype(bf16)
             return 0
 
-        lax.fori_loop(0, half // 32, chunk, 0)
+        lax.fori_loop(0, half // 32, chunk, 0, unroll=True)
         xcopy(m).start()
 
     def agcopy(l, kind, m):
@@ -412,7 +412,7 @@
             body(pl.ds(off, 32), rows, total)
             return 0
 
-        lax.fori_loop(0, half // 32, chunk, 0)
+        lax.fori_loop(0, half // 32, chunk, 0, unroll=True)
 
     def rate_of(val):
         return lax.rsqrt(jnp.mean(val * val, axis=-1, keepdims=True) + EPS)
@@ -596,9 +596,8 @@
             R[1, m, :, CA + (2 * t + 1) * U : CA + (2 * t + 2) * U] = ds[:, t * U : (t + 1) * U]
 
     def ffn_fwd(l, m, low=0, high=F // U):
-        def step(t, _):
-            off = pl.multiple_of(t * U, 128)
-            off2 = pl.multiple_of(2 * t * U, 128)
+        def step(t):
+            off, off2 = t * U, 2 * t * U
             ab = mm(L[l, N2, m], WGU[:, pl.ds(off2, 2 * U)])
             a, b = ab[:, 0:U], ab[:, U : 2 * U]
             sig = jax.nn.sigmoid(a)
@@ -610,27 +609,26 @@
                 ds = R[l, m, :, pl.ds(CA + U + off2, U)].astype(f32)
                 R[l, m, :, pl.ds(CA + off2, U)] = (ds * b * sig * (1.0 + a * (1.0 - sig))).astype(bf16)
                 R[l, m, :, pl.ds(CA + U + off2, U)] = (ds * silu).astype(bf16)
-            return 0
-
-        lax.fori_loop(low, high, step, 0)
+
+        for t in range(low, high):
+            step(t)
 
     def ffn_down(l, m):
         put_partial(m, lambda cols: mm(R[l, m, :, CS : CS + F], WD[:, cols]))
 
     def ffn_bwd(l, m):
         if l == 0:
-            def step(t, _):
-                off = pl.multiple_of(t * U, 128)
-                off2 = pl.multiple_of(2 * t * U, 128)
+            def step(t):
+                off, off2 = t * U, 2 * t * U
                 a = R[l, m, :, pl.ds(CA + off2, U)].astype(f32)
                 b = R[l, m, :, pl.ds(CA + U + off2, U)].astype(f32)
                 sig = jax.nn.sigmoid(a)
                 ds = mm(L[l, DF, m], WD[pl.ds(off, U), :], NT)
                 R[l, m, :, pl.ds(CA + off2, U)] = (ds * b * sig * (1.0 + a * (1.0 - sig))).astype(bf16)
                 R[l, m, :, pl.ds(CA + U + off2, U)] = (ds * a * sig).astype(bf16)
-                return 0
-
-            lax.fori_loop(0, F // U, step, 0)
+
+            for t in range(F // U):
+                step(t)
         put_partial(m, lambda cols: mm(R[l, m, :, CA : CA + 2 * F], WGU[cols, :], NT))
 
     def conv_bwd_a(l, m):
@@ -877,13 +875,14 @@
     def o0(m, _):
         conv_fwd_b(0, m)
         pl.when(m < M - 1)(lambda: conv_fwd_a(0, m + 1))
-        behind(None, end_o0, m)
+        pl.when(m >= 2)(lambda: end_o0(m - 2))
         gather_dyn(0, m, 0)
 
         @pl.when(m == 0)
         def _():
             arrived([load_og, load_down(1)])
 
+        mid(m)
         down_back(m)
         gather_dyn(0, m, 1)
         return 0
@@ -899,7 +898,6 @@
         pl.when(m == 0)(lambda: load_down(0).wait())
         ffn_down(0, m)
         gather_dyn(2 * M, m, 0)
-        mid(lax.rem(m + M - 1, M))
 
         @pl.when(m == M - 1)
         def _():
@@ -908,6 +906,7 @@
 
         pl.when(m < 2)(lambda: end_o0(m + M - 2))
         pl.when(m >= 2)(lambda: end_f0(m - 2))
+        mid(m)
         gather_dyn(2 * M, m, 1)
         return 0
 
@@ -920,7 +919,6 @@
         ffn_fwd(1, m)
 
     def o1(m, _):
-        pl.when(m == 0)(lambda: mid(M - 1))
         conv_fwd_b(1, m)
         pl.when(m < M - 1)(lambda: conv_fwd_a(1, m + 1))
         end_o1(m)

time: 277 us -> 271 us (0.978)
  Pallas kernels: 276 us -> 270 us
    pallas_call x1, Pallas kernels: 270 us -> 263 us  [fused_call(): pl.pallas_call(functools.partial(fused, (M, TOK, D, C, F, U)), out_shape=...]
where the time goes in v5:
time: 271 us
  Pallas kernels  270 us (100%)
    pallas_call x1, Pallas kernels, fused_call(): pl.pallas_call(functools.partial(fused, (M, TOK, D, C, F, U)), out_shape=...  263 us
    pallas_call x1, Pallas kernels, hand_on(): pl.pallas_call(functools.partial(handed_on, kinds), out_shape=[jax.ShapeD...  6.79 us

profile of v5, /device:TPU:0, one launch (start us, length us, event | category | flops | bytes accessed | tf_op | source)
XLA Modules:
  0.0 270.5 jit_solution(11710923209432475300)
XLA Ops:
  0.6 262.9 %fused.1 = (bf16[4,256,1024]{2,1,0:T(8,128)(2,1)}, bf16[4,256,1024]{2,1,0:T(8,128)(2,1)}, f32[2,256]{1,0:T(2,128)}, bf16[2,3,128,256]{3,2,1,0:T(8,128)(2,1)}, f3...) custom-call(bf16[4,256,1024]{2,1,0:T(8,128)(2,1)} %stream_in.1, ...), custom_call_target="tpu_custom_call" | custom-call | tf_op jit(solution)/shard_map/fused/pallas_call | solution.py:1059
  263.6 6.8 %hand_on.1 = (bf16[4,256,1024]{2,1,0:T(8,128)(2,1)}, f32[4,256,1024]{2,1,0:T(8,128)}, f32[2,256]{1,0:T(2,128)}, f32[2,3,128,256]{3,2,1,0:T(8,128)}, f32[3,2,256]...) custom-call(bf16[4,256,1024]{2,1,0:T(8,128)(2,1)} %get-tuple-element, ...), custom_call_target="tpu_custom_call" | custom-call | tf_op jit(solution)/shard_map/hand_on/pallas_call | solution.py:1165

commit v6 on v5

--- a/solution.py
+++ b/solution.py
@@ -251,7 +251,7 @@
     stream_in, norm_gain, win, taps, wout, ffn_gain, wgate, wup, wdown, out_grad,
     out_stream, out_sgrad, out_norm, out_in, out_conv, out_out, out_ffn, out_gate, out_up, out_down,
     L, R, WIN, WOUT, WGU, WD, H, DH, RATE, PB, PR, XR,
-    GA, GB, RA0, RA1, RA2, RB0, RB1, RB2, RT, FO, FT, SM,
+    GA, GB, RA0, RA1, RA2, RB0, RB1, RB2, RT, FO, FT, RZ, zs, zr, SM,
     EXT, DYE, CF, HALO, HALO2, DHALO, GAIN, TAPS, TAPS2, GACC, CACC, SMR,
     GAIN_IN, FGAIN_IN, TAPS_IN, NORM_OUT, FFN_OUT, CONV_OUT,
     load_sem, ps, pr, xs, xr, ags, agr, hs, dhs, hr, hs2, hr2, gs, gr, rss, rsr, fos, oss, sts, str_, sms, smr,
@@ -266,6 +266,8 @@
     table += [(0, k * U, U) for k in range(PER)]
     table += [(0, k, 128) for k in range(PER * U, CZ + C, 128)]
     UNITS = len(table)
+    LAST = UNITS - 1
+    whole = (128, 128, 0)
     splits = {w: (w, w - w // 4, w // 4) for w in (128, 256, U)}
     seq = lax.axis_index("seq")
     tp = lax.axis_index("tp")
@@ -312,7 +314,8 @@
         cp.start()
 
     barrier = pltpu.get_barrier_semaphore()
-    others = [sib, xpart, nxt, prv] + parts
+    zcross = {"seq": n - 1 - seq + 2 * lax.rem(seq, 2) - 1, "tp": tp}
+    others = [sib, xpart, nxt, prv, zcross] + parts
     for dev in others:
         pl.semaphore_signal(barrier, inc=1, device_id=dev, device_id_type=MESH)
 
@@ -707,14 +710,45 @@
                     lo, y = q // 2, q % 2
                     block = res[:, q * 128 : (q + 1) * 128]
                     GA[slot, y * 4 + lo * 2 + j, 0:cut] = block[:cut]
-                    GB[slot, lo * 4 + y * 2 + j, 0 : wide - cut] = block[cut:]
+                    if cut < wide:
+                        GB[slot, lo * 4 + y * 2 + j, 0 : wide - cut] = block[cut:]
                 return 0
 
             lax.fori_loop(0, D // 512, step, 0)
             for lane in range(2):
-                rs_copy(lane, 0, t, rows).start()
-
-        sized(t, make)
+                if rows[1 + lane]:
+                    rs_copy(lane, 0, t, rows).start()
+
+        if isinstance(t, int) and t == LAST:
+            make(whole)
+        else:
+            sized(t, make)
+
+    def last_copies():
+        base = bits[0] * 4
+        for i, (flip, dev) in enumerate(((1, parts[2]), (2, parts[1]), (3, zcross))):
+            to = (bits[1] if flip < 2 else 1 - bits[1]) * 2 + (bits[2] if flip == 2 else 1 - bits[2])
+            yield remote(GA.at[LAST % SLOTS, base + to, pl.ds(0, 128)], RZ.at[i], zs.at[i], zr.at[i], dev)
+
+    def last_add():
+        slot = LAST % SLOTS
+        rs_copy(0, 0, LAST, whole).wait()
+        base = keep(0, 0)
+        for i in range(4):
+            GA[slot, base + i, 0:128] = (
+                GA[slot, base + i, 0:128].astype(f32) + RA0[slot, i, 0:128].astype(f32)
+            ).astype(bf16)
+        for cp in last_copies():
+            cp.start()
+
+    def last_sum():
+        unit_wait(LAST - 1)
+        for cp in last_copies():
+            cp.wait()
+        total = GA[LAST % SLOTS, keep(0, 2), 0:128].astype(f32) + RZ[0].astype(f32)
+        FO[0:128] = (total + (RZ[1].astype(f32) + RZ[2].astype(f32))).astype(bf16)
+        for cp in unit_copies(LAST, 5, 128):
+            cp.start()
 
     def rs_add(step, t):
         slot = rem(t, SLOTS)
@@ -823,8 +857,10 @@
         steps = (functools.partial(rs_add, 0), functools.partial(rs_add, 1), rs_last)
         for lag, fn in enumerate(steps, 1):
             if isinstance(t, int):
-                if 0 <= t - lag < UNITS:
+                if 0 <= t - lag < LAST:
                     fn(t - lag)
+                elif t - lag == LAST and lag == 1:
+                    last_add()
             else:
                 pl.when(t >= lag)(functools.partial(fn, t - lag))
 
@@ -1033,11 +1069,12 @@
     ]
     for cp in small_out:
         cp.start()
-    while t < UNITS + 3:
+    while t < UNITS + 2:
         tick_gen(t)
         tick_rest(t)
         t += 1
-    unit_wait(UNITS - 1)
+    last_sum()
+    unit_wait(LAST)
     for cp in small_out:
         cp.wait()
     for m in range(M):
@@ -1096,6 +1133,9 @@
             vm((U, M * TOK), bf16),
             vm((U, 128), bf16),
             vm((128, U), bf16),
+            vm((3, 128, 128), bf16),
+            dma((3,)),
+            dma((3,)),
             vm((8, D), f32),
             vm((TOK + 8, C), f32),
             vm((2, TOK + 8, C), f32),
@@ -1143,7 +1183,7 @@
         first.wait()
         if kinds[i]:
             ref, wide = bufs[i].at[k], wides[i].at[k]
-            rows = 64
+            rows = 128
             lead = ref.shape[:-2]
 
             def step(r, _):
@@ -1152,7 +1192,7 @@
                 wide[at] = ref[at].astype(f32)
                 return 0
 
-            lax.fori_loop(0, (lead[0] if lead else 1) * ref.shape[-2] // rows, step, 0)
+            lax.fori_loop(0, (lead[0] if lead else 1) * ref.shape[-2] // rows, step, 0, unroll=True)
         second.start()
     for cp in outs:
         cp.wait()

time: 271 us -> 269 us (level)
  no operation moved by 1% of the time
where the time goes in v6:
time: 269 us
  Pallas kernels  268 us (100%)
    pallas_call x1, Pallas kernels, fused_call(): pl.pallas_call(functools.partial(fused, (M, TOK, D, C, F, U)), out_shape=...  262 us
    pallas_call x1, Pallas kernels, hand_on(): pl.pallas_call(functools.partial(handed_on, kinds), out_shape=[jax.ShapeD...  6.62 us

profile of v6, /device:TPU:0, one launch (start us, length us, event | category | flops | bytes accessed | tf_op | source)
XLA Modules:
  0.0 269.1 jit_solution(6259363972975551303)
XLA Ops:
  0.6 261.6 %fused.1 = (bf16[4,256,1024]{2,1,0:T(8,128)(2,1)}, bf16[4,256,1024]{2,1,0:T(8,128)(2,1)}, f32[2,256]{1,0:T(2,128)}, bf16[2,3,128,256]{3,2,1,0:T(8,128)(2,1)}, f3...) custom-call(bf16[4,256,1024]{2,1,0:T(8,128)(2,1)} %stream_in.1, ...), custom_call_target="tpu_custom_call" | custom-call | tf_op jit(solution)/shard_map/fused/pallas_call | solution.py:1096
  262.3 6.6 %hand_on.1 = (bf16[4,256,1024]{2,1,0:T(8,128)(2,1)}, f32[4,256,1024]{2,1,0:T(8,128)}, f32[2,256]{1,0:T(2,128)}, f32[2,3,128,256]{3,2,1,0:T(8,128)}, f32[3,2,256]...) custom-call(bf16[4,256,1024]{2,1,0:T(8,128)(2,1)} %get-tuple-element, ...), custom_call_target="tpu_custom_call" | custom-call | tf_op jit(solution)/shard_map/hand_on/pallas_call | solution.py:1205

commit v7 on v6

--- a/solution.py
+++ b/solution.py
@@ -253,7 +253,7 @@
     L, R, WIN, WOUT, WGU, WD, H, DH, RATE, PB, PR, XR,
     GA, GB, RA0, RA1, RA2, RB0, RB1, RB2, RT, FO, FT, RZ, zs, zr, SM,
     EXT, DYE, CF, HALO, HALO2, DHALO, GAIN, TAPS, TAPS2, GACC, CACC, SMR,
-    GAIN_IN, FGAIN_IN, TAPS_IN, NORM_OUT, FFN_OUT, CONV_OUT,
+    NORM_OUT, FFN_OUT, CONV_OUT,
     load_sem, ps, pr, xs, xr, ags, agr, hs, dhs, hr, hs2, hr2, gs, gr, rss, rsr, fos, oss, sts, str_, sms, smr,
 ):
     M, TOK, D, C, F, U = dims
@@ -319,19 +319,11 @@
     for dev in others:
         pl.semaphore_signal(barrier, inc=1, device_id=dev, device_id_type=MESH)
 
-    small_in = [
-        pltpu.make_async_copy(src, dst, load_sem.at[16 + i])
-        for i, (src, dst) in enumerate(((norm_gain, GAIN_IN), (ffn_gain, FGAIN_IN), (taps, TAPS_IN)))
-    ]
-    for cp in small_in:
-        cp.start()
-    for cp in small_in:
-        cp.wait()
-    GAIN[0] = GAIN_IN[...].astype(f32)
-    GAIN[1] = FGAIN_IN[...].astype(f32)
-    GAIN[2] = 1.0 / GAIN_IN[...].astype(f32)
-    GAIN[3] = 1.0 / FGAIN_IN[...].astype(f32)
-    TAPS[...] = TAPS_IN[...].astype(f32)
+    GAIN[0] = norm_gain[...].astype(f32)
+    GAIN[1] = ffn_gain[...].astype(f32)
+    GAIN[2] = 1.0 / norm_gain[...].astype(f32)
+    GAIN[3] = 1.0 / ffn_gain[...].astype(f32)
+    TAPS[...] = taps[...].astype(f32)
     GACC[...] = jnp.zeros_like(GACC)
     CACC[...] = jnp.zeros_like(CACC)
 
@@ -907,12 +899,13 @@
         cp.start()
 
     conv_fwd_a(0, jnp.int32(0))
+    gather_at(0)
 
     def o0(m, _):
         conv_fwd_b(0, m)
         pl.when(m < M - 1)(lambda: conv_fwd_a(0, m + 1))
         pl.when(m >= 2)(lambda: end_o0(m - 2))
-        gather_dyn(0, m, 0)
+        gather_dyn(1, m, 0)
 
         @pl.when(m == 0)
         def _():
@@ -920,7 +913,7 @@
 
         mid(m)
         down_back(m)
-        gather_dyn(0, m, 1)
+        gather_dyn(1, m, 1)
         return 0
 
     lax.fori_loop(0, M, o0, 0)
@@ -933,7 +926,7 @@
         ffn_fwd(0, m)
         pl.when(m == 0)(lambda: load_down(0).wait())
         ffn_down(0, m)
-        gather_dyn(2 * M, m, 0)
+        gather_dyn(2 * M + 1, m, 0)
 
         @pl.when(m == M - 1)
         def _():
@@ -943,7 +936,7 @@
         pl.when(m < 2)(lambda: end_o0(m + M - 2))
         pl.when(m >= 2)(lambda: end_f0(m - 2))
         mid(m)
-        gather_dyn(2 * M, m, 1)
+        gather_dyn(2 * M + 1, m, 1)
         return 0
 
     lax.fori_loop(0, M, f0, 0)
@@ -1093,6 +1086,7 @@
     dma = pltpu.SemaphoreType.DMA
     S = SLOTS
     anys = pl.BlockSpec(memory_space=pl.ANY)
+    vmem = pl.BlockSpec(memory_space=pltpu.VMEM)
     return pl.pallas_call(
         functools.partial(fused, (M, TOK, D, C, F, U)),
         out_shape=[
@@ -1107,7 +1101,7 @@
             jax.ShapeDtypeStruct((LAYERS, 128, F), bf16),
             jax.ShapeDtypeStruct((LAYERS, F, 128), bf16),
         ],
-        in_specs=[anys] * 10,
+        in_specs=[anys, vmem, anys, vmem, anys, vmem, anys, anys, anys, anys],
         out_specs=[anys] * 10,
         scratch_shapes=[
             vm((LAYERS, 4, M, TOK, D), bf16),
@@ -1149,9 +1143,6 @@
             vm((4, 8, D), f32),
             vm((LAYERS, 3, 8, C), f32),
             vm((4, 8, D), f32),
-            vm((LAYERS, D), bf16),
-            vm((LAYERS, D), bf16),
-            vm((3, LAYERS, C), bf16),
             vm((LAYERS, C), f32),
             vm((LAYERS, C), f32),
             vm((3, LAYERS, C), f32),
@@ -1168,14 +1159,19 @@
     )(stream_in, norm_gain, win, taps, wout, ffn_gain, wgate, wup, wdown, out_grad)
 
 
-def handed_on(kinds, *refs):
+def handed_on(kinds, split, *refs):
     count = len(kinds)
     srcs, dsts, bufs, wides = (refs[k * count : (k + 1) * count] for k in range(4))
     sin, sout = refs[-2:]
-    chunks = [(i, k) for i in range(count) for k in range(srcs[i].shape[0])]
-    ins = [pltpu.make_async_copy(srcs[i].at[k], bufs[i].at[k], sin.at[i, k]) for i, k in chunks]
+    chunks = [(i, k) for i in range(count) for k in (range(srcs[i].shape[0]) if i in split else (0,))]
+
+    def part(ref, i, k):
+        return ref.at[k] if i in split else ref
+
+    ins = [pltpu.make_async_copy(part(srcs[i], i, k), part(bufs[i], i, k), sin.at[i, k]) for i, k in chunks]
     outs = [
-        pltpu.make_async_copy((wides if kinds[i] else bufs)[i].at[k], dsts[i].at[k], sout.at[i, k]) for i, k in chunks
+        pltpu.make_async_copy(part((wides if kinds[i] else bufs)[i], i, k), part(dsts[i], i, k), sout.at[i, k])
+        for i, k in chunks
     ]
     for cp in ins:
         cp.start()
@@ -1202,8 +1198,9 @@
     anys = pl.BlockSpec(memory_space=pl.ANY)
     most = max(a.shape[0] for a in arrays)
     kinds = tuple(a.dtype != t for a, t in zip(arrays, types))
+    split = tuple(i for i, a in enumerate(arrays) if a.size > 16384)
     return pl.pallas_call(
-        functools.partial(handed_on, kinds),
+        functools.partial(handed_on, kinds, split),
         out_shape=[jax.ShapeDtypeStruct(a.shape, t) for a, t in zip(arrays, types)],
         in_specs=[anys] * len(arrays),
         out_specs=[anys] * len(arrays),

time: 269 us -> 269 us (level)
  no operation moved by 1% of the time
where the time goes in v7:
time: 269 us; the launch traced here: 268 us
  Pallas kernels  268 us (100%)
    pallas_call x1, Pallas kernels, fused_call(): pl.pallas_call(functools.partial(fused, (M, TOK, D, C, F, U)), out_shape=...  261 us
    pallas_call x1, Pallas kernels, hand_on(): pl.pallas_call(functools.partial(handed_on, kinds, split), out_shape=[jax...  6.58 us

profile of v7, /device:TPU:0, one launch (start us, length us, event | category | flops | bytes accessed | tf_op | source)
XLA Modules:
  0.0 268.5 jit_solution(11386546068186794966)
XLA Ops:
  0.6 261.1 %fused.1 = (bf16[4,256,1024]{2,1,0:T(8,128)(2,1)}, bf16[4,256,1024]{2,1,0:T(8,128)(2,1)}, f32[2,256]{1,0:T(2,128)}, bf16[2,3,128,256]{3,2,1,0:T(8,128)(2,1)}, f3...) custom-call(bf16[4,256,1024]{2,1,0:T(8,128)(2,1)} %stream_in.1, ...), custom_call_target="tpu_custom_call" | custom-call | tf_op jit(solution)/shard_map/fused/pallas_call | solution.py:1090
  261.7 6.6 %hand_on.1 = (bf16[4,256,1024]{2,1,0:T(8,128)(2,1)}, f32[4,256,1024]{2,1,0:T(8,128)}, f32[2,256]{1,0:T(2,128)}, f32[2,3,128,256]{3,2,1,0:T(8,128)}, f32[3,2,256]...) custom-call(bf16[4,256,1024]{2,1,0:T(8,128)(2,1)} %get-tuple-element, ...), custom_call_target="tpu_custom_call" | custom-call | tf_op jit(solution)/shard_map/hand_on/pallas_call | solution.py:1202

commit v8 on v7

--- a/solution.py
+++ b/solution.py
@@ -1041,6 +1041,11 @@
     t += 2
     for i in range(4):
         tick_gen(t)
+        tick_rest(t)
+        t += 1
+        while i == 3 and t < UNITS + 2:
+            tick_rest(t)
+            t += 1
         small(i).wait()
         if i == 0:
             SM[0:4] += SMR[0, 0:4]
@@ -1048,8 +1053,6 @@
             SM[...] += SMR[i]
         if i < 3:
             small(i + 1).start()
-        tick_rest(t)
-        t += 1
     own = pl.ds(pl.multiple_of(tp * C, 128), C)
     NORM_OUT[...] = SM[0:2, own]
     FFN_OUT[...] = SM[2:4, own]
@@ -1062,10 +1065,6 @@
     ]
     for cp in small_out:
         cp.start()
-    while t < UNITS + 2:
-        tick_gen(t)
-        tick_rest(t)
-        t += 1
     last_sum()
     unit_wait(LAST)
     for cp in small_out:
@@ -1164,6 +1163,7 @@
     srcs, dsts, bufs, wides = (refs[k * count : (k + 1) * count] for k in range(4))
     sin, sout = refs[-2:]
     chunks = [(i, k) for i in range(count) for k in (range(srcs[i].shape[0]) if i in split else (0,))]
+    chunks.sort(key=lambda c: -dsts[c[0]].size * (2 if kinds[c[0]] else 1))
 
     def part(ref, i, k):
         return ref.at[k] if i in split else ref

time: 269 us -> 268 us (level)
  no operation moved by 1% of the time
where the time goes in v8:
time: 268 us
  Pallas kernels  267 us (100%)
    pallas_call x1, Pallas kernels, fused_call(): pl.pallas_call(functools.partial(fused, (M, TOK, D, C, F, U)), out_shape=...  260 us
    pallas_call x1, Pallas kernels, hand_on(): pl.pallas_call(functools.partial(handed_on, kinds, split), out_shape=[jax...  6.25 us

profile of v8, /device:TPU:0, one launch (start us, length us, event | category | flops | bytes accessed | tf_op | source)
XLA Modules:
  0.0 267.6 jit_solution(1517365741328882528)
XLA Ops:
  0.6 260.5 %fused.1 = (bf16[4,256,1024]{2,1,0:T(8,128)(2,1)}, bf16[4,256,1024]{2,1,0:T(8,128)(2,1)}, f32[2,256]{1,0:T(2,128)}, bf16[2,3,128,256]{3,2,1,0:T(8,128)(2,1)}, f3...) custom-call(bf16[4,256,1024]{2,1,0:T(8,128)(2,1)} %stream_in.1, ...), custom_call_target="tpu_custom_call" | custom-call | tf_op jit(solution)/shard_map/fused/pallas_call | solution.py:1089
  261.1 6.2 %hand_on.1 = (bf16[4,256,1024]{2,1,0:T(8,128)(2,1)}, f32[4,256,1024]{2,1,0:T(8,128)}, f32[2,256]{1,0:T(2,128)}, f32[2,3,128,256]{3,2,1,0:T(8,128)}, f32[3,2,256]...) custom-call(bf16[4,256,1024]{2,1,0:T(8,128)(2,1)} %get-tuple-element, ...), custom_call_target="tpu_custom_call" | custom-call | tf_op jit(solution)/shard_map/hand_on/pallas_call | solution.py:1202

commit v9 on v8

--- a/solution.py
+++ b/solution.py
@@ -868,7 +868,9 @@
         def step(m, _):
             if ahead is not None:
                 ahead(m)
-            if tick is not None:
+            if tick == 1:
+                pl.when(m > 0)(lambda: tick_gen(tick + m))
+            elif tick is not None:
                 tick_gen(tick + m)
             if first is not None:
                 first(m)
@@ -960,6 +962,7 @@
     agcopy(1, N2, M - 1).wait()
     ffn_fwd(1, M - 1, 0, 1)
     tick_gen(0)
+    tick_gen(1)
     ffn_fwd(1, M - 1, 1)
 
     def start_c1(m):

time: 268 us -> 267 us (level)
  no operation moved by 1% of the time
where the time goes in v9:
time: 267 us
  Pallas kernels  266 us (100%)
    pallas_call x1, Pallas kernels, fused_call(): pl.pallas_call(functools.partial(fused, (M, TOK, D, C, F, U)), out_shape=...  260 us
    pallas_call x1, Pallas kernels, hand_on(): pl.pallas_call(functools.partial(handed_on, kinds, split), out_shape=[jax...  6.25 us

profile of v9, /device:TPU:0, one launch (start us, length us, event | category | flops | bytes accessed | tf_op | source)
XLA Modules:
  0.0 267.3 jit_solution(10747384217915885569)
XLA Ops:
  0.6 260.2 %fused.1 = (bf16[4,256,1024]{2,1,0:T(8,128)(2,1)}, bf16[4,256,1024]{2,1,0:T(8,128)(2,1)}, f32[2,256]{1,0:T(2,128)}, bf16[2,3,128,256]{3,2,1,0:T(8,128)(2,1)}, f3...) custom-call(bf16[4,256,1024]{2,1,0:T(8,128)(2,1)} %stream_in.1, ...), custom_call_target="tpu_custom_call" | custom-call | tf_op jit(solution)/shard_map/fused/pallas_call | solution.py:1092
  260.8 6.2 %hand_on.1 = (bf16[4,256,1024]{2,1,0:T(8,128)(2,1)}, f32[4,256,1024]{2,1,0:T(8,128)}, f32[2,256]{1,0:T(2,128)}, f32[2,3,128,256]{3,2,1,0:T(8,128)}, f32[3,2,256]...) custom-call(bf16[4,256,1024]{2,1,0:T(8,128)(2,1)} %get-tuple-element, ...), custom_call_target="tpu_custom_call" | custom-call | tf_op jit(solution)/shard_map/hand_on/pallas_call | solution.py:1205
